TPU v7x, 1024 devices: a whole 4x8x16 slice. The times are simulated.
1024 devices in a mesh: tm: 32 (over z, core), row: 4 (over x), col: 8 (over y).
Axes of the slice: x: 4, y: 8, z: 16, core: 2. Of those that a mesh axis runs over, the one named last changes fastest.
Arguments:
- factor_inverse: bfloat16 [131072, 4096], P(('tm', 'row'), 'col'), as said below
- coupling: bfloat16 [131072, 384], P(('tm', 'col')), as said below
- arrow_block: float32 [384, 384], replicated, as said below
Outputs:
- regression_map: float32 [131072, 384], P(('tm', 'col'))
- arrow_covariance: float32 [384, 384], replicated
Inputs may be any that keep to these rules, and one draw needn't show every extreme that they name: `factor_inverse`: each block of 4096 rows is lower triangular with diagonal entries between 0.5 and 1.5. `coupling`: entries of order one. Symmetric; the whole precision matrix made of the blocks, the coupling and arrow_block is positive definite.
All inputs are finite; a program needn't handle non-finite values.
Results may differ from a plain program's by a relative error of at most 0.0003.
The roundings to bfloat16 on the way count: a program that leaves them out, or rounds other values in their place, can miss the bound.
Values may be sent and summed in bfloat16 or wider, within the bound.
No kernel may reach another device: no remote copies, remote signals or barrier semaphores. Data moves between devices by JAX's collectives and lax.ppermute only.
A program may use at most 32 MiB of HBM per device.

v0:
```python
import jax
import jax.numpy as jnp
from jax import lax
from jax.sharding import PartitionSpec as P

B = 4096


def covariance(scaled):
    factor = jnp.linalg.cholesky(scaled)
    identity = jnp.eye(scaled.shape[0], dtype=scaled.dtype)
    solved = lax.linalg.triangular_solve(factor, identity, left_side=True, lower=True)
    return jnp.dot(solved.T, solved, precision=lax.Precision.HIGHEST)


def per_device(factor_inverse, coupling, arrow_block):
    share = lax.psum_scatter(
        jnp.dot(factor_inverse, coupling, preferred_element_type=jnp.float32),
        "col",
        scatter_dimension=0,
        tiled=True,
    )
    share_weights = share.astype(jnp.bfloat16)
    gathered = lax.all_gather(share_weights, "col", axis=0, tiled=True)
    contract = (((0,), (0,)), ((), ()))
    local_gram = lax.dot_general(
        share_weights, share_weights, contract, preferred_element_type=jnp.float32
    )
    gram_total = lax.psum(local_gram, ("tm", "row", "col"))
    mapped_part = lax.dot_general(
        factor_inverse, gathered, contract, preferred_element_type=jnp.float32
    )
    mapped = lax.psum(mapped_part, "row")
    rows_total = lax.axis_size("tm") * B
    scaled = (arrow_block - gram_total) / rows_total
    return (-mapped, covariance(scaled))


def solution(mesh):
    placed = (P(("tm", "row"), "col"), P(("tm", "col"), None), P())
    return jax.shard_map(
        per_device,
        mesh=mesh,
        in_specs=placed,
        out_specs=(P(("tm", "col"), None), P()),
        check_vma=False,
    )
```

profile of v0, /device:TPU:1, one launch (start us, length us, event | category | flops | bytes accessed | tf_op | source)
XLA Modules:
  0.0 663.8 jit_solution(17644207208688934321)
XLA Ops:
  7.2 0.0 copy-start
  7.2 0.0 copy-start.1
  7.2 0.0 reduce-scatter.2.cloned.1.call-start
  7.2 1.2 copy-done
  8.4 2.9 fusion.27
  11.2 0.0 reduce-scatter.2.cloned.1.call-update
  11.3 0.0 all-reduce.6.cloned.1.call-start
  11.3 0.0 copy-done.1
  11.3 0.2 copy.6
  11.6 0.6 iota_multiply_fusion
  12.2 52.4 %reduce-scatter.2.cloned.1.call-done = f32[128,384]{1,0:T(8,128)} async-done(((f32[1024,384]{1,0:T(8,128)}), f32[128,384]{1,0:T(8,128)}) %reduce-scatter.2.cloned.1.call-update) | async-done | bytes 196624 | tf_op jit(solution)/shard_map/reduce_scatter | solution.py:17
  64.6 0.9 convert_element_type.8
  65.6 1.1 fusion.28
  66.7 0.0 all-reduce.6.cloned.1.call-update
  66.7 0.0 all-reduce.4.cloned.1.call-start
  66.8 20.9 %all_gather.3 = bf16[1024,384]{1,0:T(8,128)(2,1)S(1)} all-gather(bf16[128,384]{1,0:T(8,128)(2,1)S(1)} %convert_element_type.8), channel_id=1, replica_groups=mesh['tm'=32,'row'=4,'col'=8] {'col'}, dimensions={0}, use_global_device_ids=true | all-gather | bytes 884736 | tf_op jit(solution)/shard_map/all_gather | solution.py:24
  87.7 1.5 convolution_bitcast_fusion
  89.2 0.0 all-reduce.4.cloned.1.call-update
  89.2 462.8 %all-reduce.6.cloned.1.call-done = f32[384,384]{0,1:T(8,128)} async-done(((f32[384,384]{0,1:T(8,128)}), f32[384,384]{0,1:T(8,128)}) %all-reduce.6.cloned.1.call-update) | async-done | bytes 589840 | tf_op jit(solution)/shard_map/psum | solution.py:29
  552.0 1.1 subtract_multiply_fusion
  553.1 0.2 copy.7
  553.3 0.1 fusion.6
  553.4 11.7 %cholesky.77 = f32[128,128]{1,0:T(8,128)S(1)} custom-call(f32[128,128]{1,0:T(8,128)S(1)} %cholesky.192), custom_call_target="Cholesky" | custom-call | tf_op jit(solution)/shard_map/jit(cholesky)/cholesky | solution.py:10
  565.2 9.8 %custom-call.22 = f32[1,128,128]{1,2,0:T(8,128)S(1)} custom-call(f32[1,128,128]{2,1,0:T(8,128)S(1)} %get-tuple-element.28), custom_call_target="InvertDiagBlocksLowerTriangular" | custom-call | tf_op jit(solution)/shard_map/jit(cholesky)/cholesky | solution.py:10
  575.0 0.0 copy-start.2
  575.1 0.3 constant_dynamic-update-slice_fusion.2
  575.3 0.3 convolution_subtract_fusion.2
  575.6 11.7 %cholesky.162 = f32[128,128]{1,0:T(8,128)S(1)} custom-call(f32[128,128]{1,0:T(8,128)S(1)} %cholesky.196), custom_call_target="Cholesky" | custom-call | tf_op jit(solution)/shard_map/jit(cholesky)/cholesky | solution.py:10
  587.4 10.0 %custom-call.23 = f32[1,128,128]{1,2,0:T(8,128)S(1)} custom-call(f32[1,128,128]{2,1,0:T(8,128)S(1)} %get-tuple-element.25), custom_call_target="InvertDiagBlocksLowerTriangular" | custom-call | tf_op jit(solution)/shard_map/jit(cholesky)/cholesky | solution.py:10
  597.3 0.2 convolution_dynamic-update-slice_fusion
  597.6 0.3 convolution_subtract_fusion.3
  597.8 11.7 %cholesky.181 = f32[128,128]{1,0:T(8,128)S(1)} custom-call(f32[128,128]{1,0:T(8,128)S(1)} %convolution_subtract_fusion.3), custom_call_target="Cholesky" | custom-call | tf_op jit(solution)/shard_map/jit(cholesky)/cholesky | solution.py:10
  609.6 0.7 compare_reduce_fusion
  610.3 0.7 compare_reduce_fusion.1
  612.9 0.0 copy-done.2
  612.9 7.8 %while.1 = (s32[]{:T(128)}, f32[384,384]{1,0:T(8,128)S(1)}, s32[3,2]{0,1:T(2,128)S(1)}, f32[3,128,128]{2,1,0:T(8,128)}, s32[]{:T(128)}) while((s32[]{:T(128)}, f32[384,384]{1,0:T(8,128)S(1)}, s32[3,2]{0,1:T(2,128)S(1)}, f32[3,128,128]{2,1,0:T(8,128)}, s32[]{:T(128)}) %tuple.30), condition=%wide.while_cond, body=%wide.while_body.sunk | while | flops 2 | bytes 132705 | solution.py:12
  612.9 0.1 constant_dynamic-slice_fusion.2
  613.0 0.5 fusion.40
  613.5 2.0 bitcast_dynamic-update-slice_fusion.2
  615.5 0.1 constant_dynamic-slice_fusion.2
  615.6 0.5 fusion.40
  616.1 2.0 bitcast_dynamic-update-slice_fusion.2
  618.1 0.1 constant_dynamic-slice_fusion.2
  618.2 0.5 fusion.40
  618.7 2.0 bitcast_dynamic-update-slice_fusion.2
  620.7 30.3 %custom-call.24 = f32[3,128,128]{1,2,0:T(8,128)S(1)} custom-call(f32[3,128,128]{2,1,0:T(8,128)} %get-tuple-element.9), custom_call_target="InvertDiagBlocksLowerTriangular" | custom-call | tf_op jit(solution)/shard_map/triangular_solve | solution.py:12
  651.0 0.3 fusion.10
  651.4 0.3 convolution_subtract_fusion.1
  651.7 0.4 fusion.19
  652.0 0.4 convolution_subtract_fusion
  652.4 0.4 fusion.17
  652.8 2.1 fusion
  655.0 0.0 all-reduce.4.cloned.1.call-done
  655.0 1.2 neg.3
  656.2 1.1 copy.8
  (11 shorter events, 0.3 us)
Async XLA Ops:
  7.2 1.2 copy-start
  7.2 4.2 copy-start.1
  7.2 57.4 %reduce-scatter.2.cloned.1.call-start = ((), (), s32[]{:S(2)}) async-start(), calls=%async_computation.1 | async-start | bytes 1769472 | tf_op jit(solution)/shard_map/reduce_scatter | solution.py:17
  11.3 540.7 %all-reduce.6.cloned.1.call-start = ((), (), s32[]{:S(2)}) async-start(), calls=%async_computation.3 | async-start | bytes 1179648 | tf_op jit(solution)/shard_map/psum | solution.py:29
  66.7 588.2 %all-reduce.4.cloned.1.call-start = ((), (), s32[]{:S(2)}) async-start(), calls=%async_computation.2 | async-start | bytes 1572864 | tf_op jit(solution)/shard_map/psum | solution.py:33
  575.0 37.8 %copy-start.2 = (s32[3]{0:T(128)S(1)}, s32[3]{0:T(128)}, u32[]{:S(2)}) copy-start(s32[3]{0:T(128)} %iota_multiply_fusion) | copy-start | bytes 40
Sparse Core Ops, SparseCore 0:
  11.5 53.1 reduce-scatter.1
  70.7 481.2 all-reduce.5
  554.9 62.0 all-reduce.3
where the time goes:
time: 666 us; the launch traced here: 664 us
  waiting for transfers between devices  515 us (77%)
  other arithmetic  90.7 us (14%)
  blocking collectives  20.9 us (3%)
  between operations  15.9 us (2%)
  local copies, waits for them, and re-layouts  10.7 us (2%)
  matrix products  10.3 us (2%)
    psum x1, waiting for transfers between devices, per_device(): gram_total = lax.psum(local_gram, ('tm', 'row', 'col'))  463 us
    another operation x10, other arithmetic, covariance(): factor = jnp.linalg.cholesky(scaled)  56.3 us
    reduce_scatter x1, waiting for transfers between devices, per_device(): lax.psum_scatter(jnp.dot(factor_inverse, coupling, preferred_element_type...  52.4 us
    another operation x3, other arithmetic, covariance(): lax.linalg.triangular_solve(factor, identity, left_side=True, lower=True)  30.9 us
    all_gather x1, blocking collectives, per_device(): gathered = lax.all_gather(share_weights, 'col', axis=0, tiled=True)  20.9 us
  transfers between devices with their start and end apart: 3, of which 2 were waited for; matrix products, arithmetic and copies ran while one was open for 16% of the time, Pallas kernels for 0%

commit v1 on v0

v1 whole, which is shorter than its diff:
```python
import jax
import jax.numpy as jnp
from jax import lax
from jax.sharding import Mesh, PartitionSpec as P

B = 4096
PLANE = ("core", "row", "col")


def covariance(scaled):
    factor = jnp.linalg.cholesky(scaled)
    identity = jnp.eye(scaled.shape[0], dtype=scaled.dtype)
    solved = lax.linalg.triangular_solve(factor, identity, left_side=True, lower=True)
    return jnp.dot(solved.T, solved, precision=lax.Precision.HIGHEST)


def spread(x, axes):
    copies = jnp.broadcast_to(x[None], (lax.axis_size(axes),) + x.shape)
    return lax.all_to_all(copies, axes, 0, 0, tiled=True)


def pack(gram):
    n = gram.shape[0] // 3
    return jnp.concatenate(
        [gram[:n], jnp.concatenate([gram[n : 2 * n, n:], gram[2 * n :, 2 * n :]], axis=1)]
    )


def unpack(packed):
    n = packed.shape[0] // 2
    a, b, c = (packed[:n, i * n : (i + 1) * n] for i in range(3))
    d, e, f = (packed[n:, i * n : (i + 1) * n] for i in range(3))
    return jnp.block([[a, b, c], [b.T, d, e], [c.T, e.T, f]])


def gram_sum(local_gram):
    plane = lax.axis_size(("core", "row"))
    cols = lax.axis_size("col")
    packed = pack(local_gram)
    rows, width = packed.shape
    piece = rows // (plane * cols)
    mine = lax.dynamic_index_in_dim(
        packed.reshape(plane, cols, piece, width), lax.axis_index("col"), 1, keepdims=False
    )
    part = jnp.sum(lax.all_to_all(mine, ("core", "row"), 0, 0, tiled=True), axis=0)
    total = jnp.sum(spread(part, "z"), axis=0)
    return unpack(spread(total, PLANE).reshape(rows, width))


def per_device(factor_inverse, coupling, arrow_block):
    share = lax.psum_scatter(
        jnp.dot(factor_inverse, coupling, preferred_element_type=jnp.float32),
        "col",
        scatter_dimension=0,
        tiled=True,
    )
    gathered = spread(share.astype(jnp.bfloat16), "col")
    gathered = gathered.reshape(-1, gathered.shape[-1])
    contract = (((0,), (0,)), ((), ()))
    mapped_part = lax.dot_general(
        factor_inverse, gathered, contract, preferred_element_type=jnp.float32
    )
    mapped = lax.psum(mapped_part, "row")
    local_gram = lax.dot_general(
        gathered, gathered, contract, preferred_element_type=jnp.float32
    )
    gram_total = gram_sum(local_gram)
    rows_total = lax.axis_size("z") * lax.axis_size("core") * B
    scaled = (arrow_block - gram_total) / rows_total
    return (-mapped, covariance(scaled))


def solution(mesh):
    tm, row, col = mesh.devices.shape
    split = Mesh(mesh.devices.reshape(tm // 2, 2, row, col), ("z",) + PLANE)
    blocks = P(("z", "core", "col"), None)
    return jax.shard_map(
        per_device,
        mesh=split,
        in_specs=(P(("z", "core", "row"), "col"), blocks, P()),
        out_specs=(blocks, P()),
        check_vma=False,
    )
```

time: 666 us -> 299 us (0.45)
  waiting for transfers between devices: 515 us -> 126 us
  starting transfers between devices: 0.12 us -> 24.8 us
  blocking collectives: 20.9 us -> 13.1 us
    psum x1 -> x0, waiting for transfers between devices: 463 us -> none  [per_device(): gram_total = lax.psum(local_gram, ('tm', 'row', 'col'))]
    psum x1, waiting for transfers between devices: 0.01 us -> 42.1 us  [per_device(): mapped = lax.psum(mapped_part, 'row')]
    all_to_all x0 -> x3, waiting for transfers between devices: none -> 30.3 us  [spread(): return lax.all_to_all(copies, axes, 0, 0, tiled=True)]
    all_to_all x0 -> x3, starting transfers between devices: none -> 24.8 us  [spread(): return lax.all_to_all(copies, axes, 0, 0, tiled=True)]
    all_gather x1 -> x0, blocking collectives: 20.9 us -> none  [per_device(): gathered = lax.all_gather(share_weights, 'col', axis=0, tiled=True)]
    all_to_all x0 -> x1, blocking collectives: none -> 13.1 us  [gram_sum(): lax.all_to_all(mine, ('core', 'row'), 0, 0, tiled=True)]
  transfers between devices with their start and end apart: 3 -> 5, of which waited for: 2 -> 4; matrix products, arithmetic and copies ran while one was open for 16% -> 2% of each run, Pallas kernels for 0% -> 0%
where the time goes in v1:
time: 299 us; the launch traced here: 297 us
  waiting for transfers between devices  126 us (42%)
  other arithmetic  90.8 us (30%)
  starting transfers between devices  24.8 us (8%)
  between operations  16.2 us (5%)
  local copies, waits for them, and re-layouts  15.4 us (5%)
  blocking collectives  13.1 us (4%)
  matrix products  10.6 us (4%)
    another operation x10, other arithmetic, covariance(): factor = jnp.linalg.cholesky(scaled)  56.4 us
    reduce_scatter x1, waiting for transfers between devices, per_device(): lax.psum_scatter(jnp.dot(factor_inverse, coupling, preferred_element_type...  53.3 us
    psum x1, waiting for transfers between devices, per_device(): mapped = lax.psum(mapped_part, 'row')  42.1 us
    another operation x3, other arithmetic, covariance(): lax.linalg.triangular_solve(factor, identity, left_side=True, lower=True)  30.4 us
    all_to_all x3, waiting for transfers between devices, spread(): return lax.all_to_all(copies, axes, 0, 0, tiled=True)  30.3 us
    all_to_all x3, starting transfers between devices, spread(): return lax.all_to_all(copies, axes, 0, 0, tiled=True)  24.8 us
    all_to_all x1, blocking collectives, gram_sum(): lax.all_to_all(mine, ('core', 'row'), 0, 0, tiled=True)  13.1 us
    another operation x9, local copies, waits for them, and re-layouts  8.15 us
  transfers between devices with their start and end apart: 5, of which 4 were waited for; matrix products, arithmetic and copies ran while one was open for 2% of the time, Pallas kernels for 0%

profile of v1, /device:TPU:1, one launch (start us, length us, event | category | flops | bytes accessed | tf_op | source)
XLA Modules:
  0.0 296.7 jit_solution(6932467215422777100)
XLA Ops:
  7.2 0.0 copy-start
  7.2 0.0 reduce-scatter.2.cloned.1.call-start
  7.2 1.2 copy-done
  8.4 2.9 fusion.28
  11.2 0.0 reduce-scatter.2.cloned.1.call-update
  11.3 53.3 %reduce-scatter.2.cloned.1.call-done = f32[128,384]{1,0:T(8,128)} async-done(((f32[1024,384]{1,0:T(8,128)}), f32[128,384]{1,0:T(8,128)}) %reduce-scatter.2.cloned.1.call-update) | async-done | bytes 196624 | tf_op jit(solution)/shard_map/reduce_scatter | solution.py:51
  64.6 0.9 convert_element_type.8
  65.6 1.0 broadcast_in_dim.7
  66.5 4.8 %all-to-all-start = ((bf16[8,128,384]{2,1,0:T(8,128)(2,1)}), bf16[8,128,384]{2,1,0:T(8,128)(2,1)S(1)}, u32[]{:S(2)}, u32[]{:S(2)}) async-start(bf16[8,128,384]{2,1,0:T(8,128)(2,1)} %broadcast_in_dim.7), calls=%async_computation.1 | async-start | bytes 1572864 | tf_op jit(solution)/shard_map/all_to_all | solution.py:19
  71.3 20.0 %all-to-all-done = bf16[8,128,384]{2,1,0:T(8,128)(2,1)S(1)} async-done(((bf16[8,128,384]{2,1,0:T(8,128)(2,1)}), bf16[8,128,384]{2,1,0:T(8,128)(2,1)S(1)}, u32[]{:S(2)}, u32[]{:S(2)}) %all-to-all-start) | async-done | bytes 786464 | tf_op jit(solution)/shard_map/all_to_all | solution.py:19
  91.3 0.6 convolution_bitcast_fusion.1
  92.0 0.1 reshape.44
  92.2 13.1 %all_to_all.20 = f32[8,4,384]{2,1,0:T(4,128)S(1)} all-to-all(f32[8,4,384]{2,1,0:T(4,128)S(1)} %dynamic-slice_bitcast_fusion), channel_id=1, replica_groups=mesh['z'=16,'core'=2,'row'=4,'col'=8] {'core','row'}, dimensions={0} | all-to-all | bytes 98304 | tf_op jit(solution)/shard_map/all_to_all | solution.py:45
  105.3 0.7 broadcast_in_dim.8
  105.9 12.8 %all-to-all-start.2 = ((f32[16,4,384]{2,1,0:T(4,128)}), f32[16,4,384]{2,1,0:T(4,128)S(1)}, u32[]{:S(2)}, u32[]{:S(2)}) async-start(f32[16,4,384]{2,1,0:T(4,128)} %broadcast_in_dim.8), calls=%async_computation.3 | async-start | bytes 196608 | tf_op jit(solution)/shard_map/all_to_all | solution.py:19
  118.7 0.0 all-reduce.3.cloned.1.call-start
  118.7 1.5 convolution_bitcast_fusion
  120.2 0.0 all-reduce.3.cloned.1.call-update
  120.2 10.3 %all-to-all-done.2 = f32[16,4,384]{2,1,0:T(4,128)S(1)} async-done(((f32[16,4,384]{2,1,0:T(4,128)}), f32[16,4,384]{2,1,0:T(4,128)S(1)}, u32[]{:S(2)}, u32[]{:S(2)}) %all-to-all-start.2) | async-done | bytes 98336 | tf_op jit(solution)/shard_map/all_to_all | solution.py:19
  130.6 0.8 broadcast_in_dim.9
  131.4 7.2 %all-to-all-start.3 = ((f32[64,4,384]{2,1,0:T(4,128)}), f32[64,4,384]{2,1,0:T(4,128)S(1)}, u32[]{:S(2)}, u32[]{:S(2)}) async-start(f32[64,4,384]{2,1,0:T(4,128)} %broadcast_in_dim.9), calls=%async_computation.4 | async-start | bytes 786432 | tf_op jit(solution)/shard_map/all_to_all | solution.py:19
  138.6 0.2 copy.31
  138.9 0.7 iota_compare_fusion
  139.6 42.1 %all-reduce.3.cloned.1.call-done = f32[512,384]{0,1:T(8,128)} async-done(((f32[512,384]{0,1:T(8,128)}), f32[512,384]{0,1:T(8,128)}) %all-reduce.3.cloned.1.call-update) | async-done | bytes 786448 | tf_op jit(solution)/shard_map/psum | solution.py:63
  181.7 1.2 neg.3
  183.0 1.1 copy.33
  184.1 0.0 all-to-all-done.3
  184.1 0.1 reshape.45
  184.2 0.7 slice_bitcast_fusion.8
  184.9 0.7 copy.37
  185.6 0.1 copy.36
  185.8 0.1 slice.109
  185.8 0.1 copy.30
  186.0 1.0 fusion
  187.0 0.2 copy.32
  187.2 0.1 fusion.7
  187.3 11.7 %cholesky.77 = f32[128,128]{1,0:T(8,128)S(1)} custom-call(f32[128,128]{1,0:T(8,128)S(1)} %cholesky.192), custom_call_target="Cholesky" | custom-call | tf_op jit(solution)/shard_map/jit(cholesky)/cholesky | solution.py:11
  199.1 9.8 %custom-call.22 = f32[1,128,128]{1,2,0:T(8,128)S(1)} custom-call(f32[1,128,128]{2,1,0:T(8,128)S(1)} %get-tuple-element.38), custom_call_target="InvertDiagBlocksLowerTriangular" | custom-call | tf_op jit(solution)/shard_map/jit(cholesky)/cholesky | solution.py:11
  208.9 0.3 constant_dynamic-update-slice_fusion.2
  209.2 0.3 convolution_subtract_fusion.2
  209.5 11.7 %cholesky.162 = f32[128,128]{1,0:T(8,128)S(1)} custom-call(f32[128,128]{1,0:T(8,128)S(1)} %cholesky.196), custom_call_target="Cholesky" | custom-call | tf_op jit(solution)/shard_map/jit(cholesky)/cholesky | solution.py:11
  221.2 10.0 %custom-call.23 = f32[1,128,128]{1,2,0:T(8,128)S(1)} custom-call(f32[1,128,128]{2,1,0:T(8,128)S(1)} %get-tuple-element.35), custom_call_target="InvertDiagBlocksLowerTriangular" | custom-call | tf_op jit(solution)/shard_map/jit(cholesky)/cholesky | solution.py:11
  231.2 0.2 convolution_dynamic-update-slice_fusion
  231.4 0.3 convolution_subtract_fusion.3
  231.7 11.7 %cholesky.181 = f32[128,128]{1,0:T(8,128)S(1)} custom-call(f32[128,128]{1,0:T(8,128)S(1)} %convolution_subtract_fusion.3), custom_call_target="Cholesky" | custom-call | tf_op jit(solution)/shard_map/jit(cholesky)/cholesky | solution.py:11
  243.4 0.7 compare_reduce_fusion
  244.2 0.6 compare_reduce_fusion.1
  246.8 8.2 %while.1 = (s32[]{:T(128)}, f32[384,384]{1,0:T(8,128)S(1)}, s32[3,2]{0,1:T(2,128)S(1)}, f32[3,128,128]{2,1,0:T(8,128)}, s32[]{:T(128)}) while((s32[]{:T(128)}, f32[384,384]{1,0:T(8,128)S(1)}, s32[3,2]{0,1:T(2,128)S(1)}, f32[3,128,128]{2,1,0:T(8,128)}, s32[]{:T(128)}) %tuple.36), condition=%wide.while_cond, body=%wide.while_body.sunk | while | flops 2 | bytes 132705 | solution.py:13
  246.8 0.1 constant_dynamic-slice_fusion.2
  246.9 0.6 fusion.40
  247.5 2.0 bitcast_dynamic-update-slice_fusion.2
  249.5 0.1 constant_dynamic-slice_fusion.2
  249.6 0.6 fusion.40
  250.2 2.0 bitcast_dynamic-update-slice_fusion.2
  252.2 0.1 constant_dynamic-slice_fusion.2
  252.3 0.6 fusion.40
  252.9 2.1 bitcast_dynamic-update-slice_fusion.2
  254.9 30.3 %custom-call.24 = f32[3,128,128]{1,2,0:T(8,128)S(1)} custom-call(f32[3,128,128]{2,1,0:T(8,128)} %get-tuple-element.9), custom_call_target="InvertDiagBlocksLowerTriangular" | custom-call | tf_op jit(solution)/shard_map/triangular_solve | solution.py:13
  285.2 1.0 fusion.11
  286.3 0.3 convolution_subtract_fusion.1
  286.6 0.4 fusion.20
  287.0 0.4 convolution_subtract_fusion
  287.4 0.4 fusion.18
  287.8 2.1 fusion.1
  (22 shorter events, 0.4 us)
Async XLA Ops:
  7.2 1.2 copy-start
  7.2 57.4 %reduce-scatter.2.cloned.1.call-start = ((), (), s32[]{:S(2)}) async-start(), calls=%async_computation.5 | async-start | bytes 1769472 | tf_op jit(solution)/shard_map/reduce_scatter | solution.py:51
  66.5 24.8 %all-to-all-start = ((bf16[8,128,384]{2,1,0:T(8,128)(2,1)}), bf16[8,128,384]{2,1,0:T(8,128)(2,1)S(1)}, u32[]{:S(2)}, u32[]{:S(2)}) async-start(bf16[8,128,384]{2,1,0:T(8,128)(2,1)} %broadcast_in_dim.7), calls=%async_computation.1 | async-start | bytes 1572864 | tf_op jit(solution)/shard_map/all_to_all | solution.py:19
  105.9 24.7 %all-to-all-start.2 = ((f32[16,4,384]{2,1,0:T(4,128)}), f32[16,4,384]{2,1,0:T(4,128)S(1)}, u32[]{:S(2)}, u32[]{:S(2)}) async-start(f32[16,4,384]{2,1,0:T(4,128)} %broadcast_in_dim.8), calls=%async_computation.3 | async-start | bytes 196608 | tf_op jit(solution)/shard_map/all_to_all | solution.py:19
  118.7 63.1 %all-reduce.3.cloned.1.call-start = ((), (), s32[]{:S(2)}) async-start(), calls=%async_computation.6 | async-start | bytes 1572864 | tf_op jit(solution)/shard_map/psum | solution.py:63
  120.2 18.4 %copy-start.1 = (f32[384,384]{1,0:T(8,128)S(1)}, f32[384,384]{1,0:T(8,128)}, u32[]{:S(2)}) copy-start(f32[384,384]{1,0:T(8,128)} %param.5) | copy-start | bytes 1769476
  131.4 52.7 %all-to-all-start.3 = ((f32[64,4,384]{2,1,0:T(4,128)}), f32[64,4,384]{2,1,0:T(4,128)S(1)}, u32[]{:S(2)}, u32[]{:S(2)}) async-start(f32[64,4,384]{2,1,0:T(4,128)} %broadcast_in_dim.9), calls=%async_computation.4 | async-start | bytes 786432 | tf_op jit(solution)/shard_map/all_to_all | solution.py:19
Sparse Core Ops, SparseCore 0:
  11.4 53.1 reduce-scatter.1
  122.5 59.2 all-reduce.2

commit v2 on v0

v2 whole, which is shorter than its diff:
```python
import functools

import jax
import jax.numpy as jnp
from jax import lax
from jax.experimental import pallas as pl
from jax.experimental.pallas import tpu as pltpu
from jax.sharding import Mesh, PartitionSpec as P

B = 4096
PLANE = ("core", "row", "col")


PANEL = 8


def dot32(a, b, left=1, right=0):
    return lax.dot_general(
        a,
        b,
        (((left,), (right,)), ((), ())),
        precision=lax.Precision.HIGHEST,
        preferred_element_type=jnp.float32,
    )


def block_inverse(m):
    n, w = m.shape[0], PANEL
    lane = lax.broadcasted_iota(jnp.int32, (n, n), 1)
    panel_lane = lax.broadcasted_iota(jnp.int32, (w, n), 1)
    sub = lax.broadcasted_iota(jnp.int32, (w, n), 0)
    for k in range(0, n, w):
        rows = m[k : k + w, :]
        cols = [jnp.broadcast_to(rows[:, k + j : k + j + 1], (w, n)) for j in range(w)]
        inside = (panel_lane >= k) & (panel_lane < k + w)
        t = jnp.where(inside, jnp.where(panel_lane == sub + k, 1.0, 0.0), rows)
        for j in range(w):
            inv = 1.0 / cols[j][j : j + 1, :]
            pivot = t[j : j + 1, :] * inv
            t = jnp.where(sub == j, pivot, t - cols[j] * pivot)
            for i in range(j + 1, w):
                p = cols[i][j : j + 1, :] * inv
                cols[i] = jnp.where(sub == j, p, cols[i] - cols[j] * p)
        new = jnp.where((lane >= k) & (lane < k + w), 0.0, m)
        for j in range(w):
            new = new - m[:, k + j : k + j + 1] * t[j : j + 1, :]
        m = jnp.concatenate([x for x in (new[:k], t, new[k + w :]) if x.shape[0]])
    return m


def upper_blocks(products):
    return products[0], jnp.concatenate(products[1:], axis=1)


def weights_kernel(share_ref, copies_ref, pieces_ref):
    weights = share_ref[...].astype(jnp.bfloat16)
    for i in range(copies_ref.shape[0]):
        copies_ref[i] = -weights
    n = weights.shape[1] // 3
    contract = (((0,), (0,)), ((), ()))
    half = pieces_ref.shape[0] // 2
    piece = pieces_ref.shape[1]
    products = [
        lax.dot_general(
            weights[:, i * n : (i + 1) * n],
            weights[:, i * n :],
            contract,
            preferred_element_type=jnp.float32,
        )
        for i in range(3)
    ]
    for upper, block_row in enumerate(upper_blocks(products)):
        for i in range(half):
            pieces_ref[upper * half + i] = block_row[i * piece : (i + 1) * piece]


def sum_kernel(parts_ref, after_ref, copies_ref):
    del after_ref
    total = parts_ref[0]
    for i in range(1, parts_ref.shape[0]):
        total = total + parts_ref[i]
    for i in range(copies_ref.shape[0]):
        copies_ref[i] = total


def inverse_kernel(scale, pieces_ref, arrow_ref, after_ref, out_ref):
    del after_ref
    n = arrow_ref.shape[0] // 3
    half = pieces_ref.shape[0] // 2
    s = [slice(i * n, (i + 1) * n) for i in range(3)]

    def block(i, j):
        first, c = (0, j) if i == 0 else (half, i + j - 2)
        gram = jnp.concatenate([pieces_ref[first + p, :, s[c]] for p in range(half)])
        return (arrow_ref[s[i], s[j]] - gram) * scale

    p0 = block_inverse(block(0, 0))
    a0 = jnp.concatenate([block(0, 1), block(0, 2)], axis=1)
    t0 = dot32(p0, a0)
    low = dot32(a0, t0, 0, 0)
    p1 = block_inverse(block(1, 1) - low[:n, :n])
    a1 = block(1, 2) - low[:n, n:]
    t1 = dot32(p1, a1)
    p2 = block_inverse(block(2, 2) - low[n:, n:] - dot32(a1, t1, 0, 0))
    x12 = -dot32(t1, p2)
    x11 = p1 - dot32(x12, t1, 1, 1)
    rest = jnp.concatenate(
        [jnp.concatenate([x11, x12], axis=1), jnp.concatenate([x12.T, p2], axis=1)]
    )
    x0 = -dot32(t0, rest)
    out_ref[s[0], s[0]] = p0 - dot32(x0, t0, 1, 1)
    out_ref[s[0], n:] = x0
    out_ref[n:, s[0]] = x0.T
    out_ref[n:, n:] = rest


VMEM = pl.BlockSpec(memory_space=pltpu.VMEM)
LATER = pl.BlockSpec(memory_space=pl.ANY)


def call(kernel, out_shape, in_specs, flops):
    return pl.pallas_call(
        kernel,
        out_shape=out_shape,
        in_specs=in_specs,
        out_specs=jax.tree.map(lambda _: VMEM, out_shape),
        compiler_params=pltpu.CompilerParams(vmem_limit_bytes=16 * 2**20),
        cost_estimate=pl.CostEstimate(flops=flops, bytes_accessed=2**20, transcendentals=0),
    )


def exchange(pieces, axes):
    return lax.all_to_all(pieces, axes, 0, 0, tiled=True)


def per_device(factor_inverse, coupling, arrow_block):
    f32 = jnp.float32
    share = lax.psum_scatter(
        jnp.dot(factor_inverse, coupling, preferred_element_type=f32),
        "col",
        scatter_dimension=0,
        tiled=True,
    )
    cols, planes, size = (lax.axis_size(a) for a in ("col", "z", PLANE))
    width = share.shape[1]
    piece = (2 * width // 3 // size, width)
    copies, pieces = call(
        weights_kernel,
        (
            jax.ShapeDtypeStruct((cols,) + share.shape, jnp.bfloat16),
            jax.ShapeDtypeStruct((size,) + piece, f32),
        ),
        [VMEM],
        10**9,
    )(share)
    parts = exchange(pieces, PLANE)
    gathered = exchange(copies, "col").reshape(-1, width)

    mapped_part = lax.dot_general(
        factor_inverse, gathered, (((0,), (0,)), ((), ())), preferred_element_type=f32
    )
    mapped_share = lax.psum_scatter(mapped_part, "row", scatter_dimension=0, tiled=True)
    rows = lax.axis_size("row")
    mapped = exchange(
        jnp.broadcast_to(mapped_share[None], (rows,) + mapped_share.shape), "row"
    ).reshape(-1, width)

    by_plane = call(
        sum_kernel, jax.ShapeDtypeStruct((planes,) + piece, f32), [VMEM, LATER], 10**7
    )(parts, copies)
    by_plane = exchange(by_plane, "z")
    totals = call(
        sum_kernel, jax.ShapeDtypeStruct((size,) + piece, f32), [VMEM, LATER], 10**7
    )(by_plane, mapped_part)
    totals = exchange(totals, PLANE)
    rows_total = planes * lax.axis_size("core") * B
    covariance = call(
        functools.partial(inverse_kernel, 1.0 / rows_total),
        jax.ShapeDtypeStruct(arrow_block.shape, f32),
        [VMEM, VMEM, LATER],
        15 * 10**9,
    )(totals, arrow_block, mapped_share)
    return (mapped, covariance)


def solution(mesh):
    tm, row, col = mesh.devices.shape
    split = Mesh(mesh.devices.reshape(tm // 2, 2, row, col), ("z",) + PLANE)
    blocks = P(("z", "core", "col"), None)
    return jax.shard_map(
        per_device,
        mesh=split,
        in_specs=(P(("z", "core", "row"), "col"), blocks, P()),
        out_specs=(blocks, P()),
        check_vma=False,
    )
```

time: 666 us -> 191 us (0.29)
  waiting for transfers between devices: 515 us -> 67.7 us
  other arithmetic: 90.7 us -> 0 us
  blocking collectives: 20.9 us -> 70.3 us
  Pallas kernels: 0 us -> 14.3 us
  starting transfers between devices: 0.12 us -> 14.2 us
    psum x2 -> x0, waiting for transfers between devices: 463 us -> none  [the longest x1 463 us: per_device(): gram_total = lax.psum(local_gram, ('tm', 'row', 'col'))]
    another operation x13 -> x0, other arithmetic: 87.3 us -> none  [the longest x10 56.3 us: covariance(): factor = jnp.linalg.cholesky(scaled)]
    all_to_all x0 -> x3, blocking collectives: none -> 70.3 us  [exchange(): return lax.all_to_all(pieces, axes, 0, 0, tiled=True)]
    all_gather x1 -> x0, blocking collectives: 20.9 us -> none  [per_device(): gathered = lax.all_gather(share_weights, 'col', axis=0, tiled=True)]
    pallas_call x0 -> x4, Pallas kernels: none -> 14.3 us  [the longest x1 13.2 us: per_device(): call(functools.partial(inverse_kernel, 1.0 / rows_total), jax.ShapeDtypeS...]
    all_to_all x0 -> x2, waiting for transfers between devices: none -> 14.3 us  [exchange(): return lax.all_to_all(pieces, axes, 0, 0, tiled=True)]
    all_to_all x0 -> x2, starting transfers between devices: none -> 14.1 us  [exchange(): return lax.all_to_all(pieces, axes, 0, 0, tiled=True)]
    another operation x13 -> x0, local copies, waits for them, and re-layouts: 7.88 us -> none
  transfers between devices with their start and end apart: 3 -> 4, of which waited for: 2 -> 2; matrix products, arithmetic and copies ran while one was open for 16% -> 1% of each run, Pallas kernels for 0% -> 7%
where the time goes in v2:
time: 191 us; the launch traced here: 190 us
  blocking collectives  70.3 us (37%)
  waiting for transfers between devices  67.7 us (35%)
  Pallas kernels  14.3 us (7%)
  starting transfers between devices  14.2 us (7%)
  between operations  14.1 us (7%)
  local copies, waits for them, and re-layouts  4.93 us (3%)
  matrix products  4.49 us (2%)
    all_to_all x3, blocking collectives, exchange(): return lax.all_to_all(pieces, axes, 0, 0, tiled=True)  70.3 us
    reduce_scatter x1, waiting for transfers between devices, per_device(): lax.psum_scatter(jnp.dot(factor_inverse, coupling, preferred_element_type...  53.3 us
    all_to_all x2, waiting for transfers between devices, exchange(): return lax.all_to_all(pieces, axes, 0, 0, tiled=True)  14.3 us
    all_to_all x2, starting transfers between devices, exchange(): return lax.all_to_all(pieces, axes, 0, 0, tiled=True)  14.1 us
    pallas_call x1, Pallas kernels, per_device(): call(functools.partial(inverse_kernel, 1.0 / rows_total), jax.ShapeDtypeS...  13.2 us
  transfers between devices with their start and end apart: 4, of which 2 were waited for; matrix products, arithmetic and copies ran while one was open for 1% of the time, Pallas kernels for 7%

profile of v2, /device:TPU:1, one launch (start us, length us, event | category | flops | bytes accessed | tf_op | source)
XLA Modules:
  0.0 190.0 jit_solution(17993322292756037963)
XLA Ops:
  7.2 0.0 copy-start
  7.2 0.0 reduce-scatter.3.cloned.1.call-start
  7.2 1.2 copy-done
  8.4 2.9 %fusion = f32[1024,384]{1,0:T(8,128)} fusion(bf16[1024,512]{1,0:T(8,128)(2,1)S(1)} %copy-done, bf16[512,384]{1,0:T(8,128)(2,1)} %param.4), kind=kOutput, calls=%fused_computation.1 | convolution fusion | flops 402653184 | bytes 3014656 | tf_op jit(solution)/shard_map/dot_general | solution.py:139
  11.2 0.0 reduce-scatter.3.cloned.1.call-update
  11.3 53.3 %reduce-scatter.3.cloned.1.call-done.share_ref = f32[128,384]{1,0:T(8,128)} async-done(((f32[1024,384]{1,0:T(8,128)}), f32[128,384]{1,0:T(8,128)}) %reduce-scatter.3.cloned.1.call-update) | async-done | bytes 196624 | tf_op jit(solution)/shard_map/reduce_scatter | solution.py:138
  64.6 0.0 copy-start.4
  64.6 0.9 copy-done.4
  65.5 1.0 shard_map.50
  66.6 23.1 %all_to_all.25 = bf16[8,128,384]{2,1,0:T(8,128)(2,1)S(1)} all-to-all(bf16[8,128,384]{2,1,0:T(8,128)(2,1)S(1)} %get-tuple-element.4.after_ref), channel_id=1, replica_groups=mesh['z'=16,'core'=2,'row'=4,'col'=8] {'col'}, dimensions={0} | all-to-all | bytes 1572864 | tf_op jit(solution)/shard_map/all_to_all | solution.py:133
  89.6 10.5 %all-to-all-start.2 = ((f32[64,4,384]{2,1,0:T(4,128)}), f32[64,4,384]{2,1,0:T(4,128)S(1)}, u32[]{:S(2)}, u32[]{:S(2)}) async-start(f32[64,4,384]{2,1,0:T(4,128)} %get-tuple-element.5), calls=%async_computation.4 | async-start | bytes 786432 | tf_op jit(solution)/shard_map/all_to_all | solution.py:133
  100.1 0.0 reduce-scatter.5.cloned.1.call-start
  100.2 1.6 convolution_bitcast_fusion.after_ref
  101.8 0.0 copy-start.1
  101.8 0.0 reduce-scatter.5.cloned.1.call-update
  101.8 14.3 %all-to-all-done.2.parts_ref = f32[64,4,384]{2,1,0:T(4,128)S(1)} async-done(((f32[64,4,384]{2,1,0:T(4,128)}), f32[64,4,384]{2,1,0:T(4,128)S(1)}, u32[]{:S(2)}, u32[]{:S(2)}) %all-to-all-start.2) | async-done | bytes 393248 | tf_op jit(solution)/shard_map/all_to_all | solution.py:133
  116.1 0.1 shard_map.51
  116.2 24.5 %all_to_all.26.parts_ref = f32[16,4,384]{2,1,0:T(4,128)S(1)} all-to-all(f32[16,4,384]{2,1,0:T(4,128)S(1)} %shard_map.51), channel_id=1, replica_groups=mesh['z'=16,'core'=2,'row'=4,'col'=8] {'z'}, dimensions={0} | all-to-all | bytes 196608 | tf_op jit(solution)/shard_map/all_to_all | solution.py:133
  140.7 0.0 copy-done.1
  140.7 0.1 shard_map.52
  140.7 0.0 copy-start.3
  140.7 22.7 %all_to_all.27.pieces_ref = f32[64,4,384]{2,1,0:T(4,128)S(1)} all-to-all(f32[64,4,384]{2,1,0:T(4,128)S(1)} %shard_map.52), channel_id=1, replica_groups=mesh['z'=16,'core'=2,'row'=4,'col'=8] {'core','row','col'}, dimensions={0} | all-to-all | bytes 786432 | tf_op jit(solution)/shard_map/all_to_all | solution.py:133
  163.5 0.0 reduce-scatter.5.cloned.1.call-done.after_ref
  163.5 0.0 copy-start.2
  163.5 1.9 %broadcast_in_dim.2 = f32[4,128,384]{2,1,0:T(8,128)} broadcast(f32[128,384]{1,0:T(8,128)} %reduce-scatter.5.cloned.1.call-done.after_ref), dimensions={1,2} | broadcast | bytes 983040 | tf_op jit(solution)/shard_map/broadcast_in_dim | solution.py:165
  165.4 3.7 %all-to-all-start.1 = ((f32[4,128,384]{2,1,0:T(8,128)}), f32[4,128,384]{2,1,0:T(8,128)S(1)}, u32[]{:S(2)}, u32[]{:S(2)}) async-start(f32[4,128,384]{2,1,0:T(8,128)} %broadcast_in_dim.2), calls=%async_computation.3 | async-start | bytes 1572864 | tf_op jit(solution)/shard_map/all_to_all | solution.py:133
  169.1 0.0 copy-done.3
  169.1 0.0 copy-done.2
  169.1 13.2 %shard_map.53 = f32[384,384]{1,0:T(8,128)} custom-call(f32[64,4,384]{2,1,0:T(4,128)S(1)} %all_to_all.27.pieces_ref, f32[384,384]{1,0:T(8,128)S(1)} %copy-done.3, f32[128,384]{1,0:T(8,128)S(1)} %copy-done.2), custom_call_target="tpu_custom_call" | custom-call | flops 15000000512 | bytes 1048576 | tf_op jit(solution)/shard_map/pallas_call | solution.py:177
  182.3 0.0 all-to-all-done.1
  182.3 0.9 copy.8
Async XLA Ops:
  7.2 1.2 copy-start
  7.2 57.4 %reduce-scatter.3.cloned.1.call-start = ((), (), s32[]{:S(2)}) async-start(), calls=%async_computation.7 | async-start | bytes 1769472 | tf_op jit(solution)/shard_map/reduce_scatter | solution.py:138
  64.6 0.9 copy-start.4
  89.6 26.5 %all-to-all-start.2 = ((f32[64,4,384]{2,1,0:T(4,128)}), f32[64,4,384]{2,1,0:T(4,128)S(1)}, u32[]{:S(2)}, u32[]{:S(2)}) async-start(f32[64,4,384]{2,1,0:T(4,128)} %get-tuple-element.5), calls=%async_computation.4 | async-start | bytes 786432 | tf_op jit(solution)/shard_map/all_to_all | solution.py:133
  100.1 63.4 %reduce-scatter.5.cloned.1.call-start = ((), (), s32[]{:S(2)}) async-start(), calls=%async_computation.8 | async-start | bytes 983040 | tf_op jit(solution)/shard_map/reduce_scatter | solution.py:162
  101.8 38.9 %copy-start.1 = (f32[512,384]{1,0:T(8,128)S(1)}, f32[512,384]{1,0:T(8,128)}, u32[]{:S(2)}) copy-start(f32[512,384]{1,0:T(8,128)} %convolution_bitcast_fusion.after_ref) | copy-start | bytes 2359300
  140.7 28.4 %copy-start.3 = (f32[384,384]{1,0:T(8,128)S(1)}, f32[384,384]{1,0:T(8,128)}, u32[]{:S(2)}) copy-start(f32[384,384]{1,0:T(8,128)} %arrow_ref.1) | copy-start | bytes 1769476
  163.5 5.6 %copy-start.2 = (f32[128,384]{1,0:T(8,128)S(1)}, f32[128,384]{1,0:T(8,128)}, u32[]{:S(2)}) copy-start(f32[128,384]{1,0:T(8,128)} %reduce-scatter.5.cloned.1.call-done.after_ref) | copy-start | bytes 589828
  165.4 16.9 %all-to-all-start.1 = ((f32[4,128,384]{2,1,0:T(8,128)}), f32[4,128,384]{2,1,0:T(8,128)S(1)}, u32[]{:S(2)}, u32[]{:S(2)}) async-start(f32[4,128,384]{2,1,0:T(8,128)} %broadcast_in_dim.2), calls=%async_computation.3 | async-start | bytes 1572864 | tf_op jit(solution)/shard_map/all_to_all | solution.py:133
Sparse Core Ops, SparseCore 0:
  11.4 53.1 reduce-scatter.2
  105.0 33.2 reduce-scatter.4

commit v3 on v2

--- a/solution.py
+++ b/solution.py
@@ -8,7 +8,7 @@
 from jax.sharding import Mesh, PartitionSpec as P
 
 B = 4096
-PLANE = ("core", "row", "col")
+PLANE = ("row", "col")
 
 
 PANEL = 8
@@ -48,30 +48,42 @@
     return m
 
 
-def upper_blocks(products):
-    return products[0], jnp.concatenate(products[1:], axis=1)
-
-
-def weights_kernel(share_ref, copies_ref, pieces_ref):
-    weights = share_ref[...].astype(jnp.bfloat16)
-    for i in range(copies_ref.shape[0]):
-        copies_ref[i] = -weights
+def gram_kernel(mine_ref, other_ref, pieces_ref):
+    weights = jnp.concatenate([mine_ref[...], other_ref[...]])
     n = weights.shape[1] // 3
-    contract = (((0,), (0,)), ((), ()))
-    half = pieces_ref.shape[0] // 2
     piece = pieces_ref.shape[1]
-    products = [
-        lax.dot_general(
+
+    def product(i):
+        return lax.dot_general(
             weights[:, i * n : (i + 1) * n],
             weights[:, i * n :],
-            contract,
+            (((0,), (0,)), ((), ())),
             preferred_element_type=jnp.float32,
         )
-        for i in range(3)
-    ]
-    for upper, block_row in enumerate(upper_blocks(products)):
-        for i in range(half):
-            pieces_ref[upper * half + i] = block_row[i * piece : (i + 1) * piece]
+
+    def store(block_row):
+        for i in range(pieces_ref.shape[0]):
+            pieces_ref[i] = block_row[i * piece : (i + 1) * piece]
+
+    core = lax.axis_index("core")
+
+    @pl.when(core == 0)
+    def _():
+        store(product(0))
+
+    @pl.when(core == 1)
+    def _():
+        store(jnp.concatenate([product(1), product(2)], axis=1))
+
+
+def map_kernel(factor_ref, sums_ref, after_ref, out_ref):
+    del after_ref
+    out_ref[...] = lax.dot_general(
+        factor_ref[...],
+        -sums_ref[...].astype(jnp.bfloat16),
+        (((0,), (0,)), ((), ())),
+        preferred_element_type=jnp.float32,
+    )
 
 
 def sum_kernel(parts_ref, after_ref, copies_ref):
@@ -83,15 +95,18 @@
         copies_ref[i] = total
 
 
-def inverse_kernel(scale, pieces_ref, arrow_ref, after_ref, out_ref):
+def inverse_kernel(scale, mine_ref, other_ref, arrow_ref, after_ref, out_ref):
     del after_ref
     n = arrow_ref.shape[0] // 3
-    half = pieces_ref.shape[0] // 2
     s = [slice(i * n, (i + 1) * n) for i in range(3)]
+    first = lax.axis_index("core") == 0
+    pieces = range(mine_ref.shape[0])
 
     def block(i, j):
-        first, c = (0, j) if i == 0 else (half, i + j - 2)
-        gram = jnp.concatenate([pieces_ref[first + p, :, s[c]] for p in range(half)])
+        c = s[j if i == 0 else i + j - 2]
+        mine = jnp.concatenate([mine_ref[p, :, c] for p in pieces])
+        other = jnp.concatenate([other_ref[p, :, c] for p in pieces])
+        gram = jnp.where(first == (i == 0), mine, other)
         return (arrow_ref[s[i], s[j]] - gram) * scale
 
     p0 = block_inverse(block(0, 0))
@@ -133,59 +148,61 @@
     return lax.all_to_all(pieces, axes, 0, 0, tiled=True)
 
 
+def swap(x):
+    return lax.ppermute(x, "core", [(0, 1), (1, 0)])
+
+
 def per_device(factor_inverse, coupling, arrow_block):
     f32 = jnp.float32
+    shape = jax.ShapeDtypeStruct
     share = lax.psum_scatter(
         jnp.dot(factor_inverse, coupling, preferred_element_type=f32),
         "col",
         scatter_dimension=0,
         tiled=True,
     )
-    cols, planes, size = (lax.axis_size(a) for a in ("col", "z", PLANE))
+    gathered = lax.all_gather(share, "col", tiled=True)
+    weights = share.astype(jnp.bfloat16)
+    planes, size, rows = (lax.axis_size(a) for a in ("z", PLANE, "row"))
     width = share.shape[1]
-    piece = (2 * width // 3 // size, width)
-    copies, pieces = call(
-        weights_kernel,
-        (
-            jax.ShapeDtypeStruct((cols,) + share.shape, jnp.bfloat16),
-            jax.ShapeDtypeStruct((size,) + piece, f32),
-        ),
-        [VMEM],
+    piece = (width // 3 // size, width)
+
+    pieces = call(gram_kernel, shape((size,) + piece, f32), [VMEM] * 2, 10**9)(
+        weights, swap(weights)
+    )
+    parts = exchange(pieces, PLANE)
+    parts = call(sum_kernel, shape((planes,) + piece, f32), [VMEM, LATER], 10**7)(parts, weights)
+    parts = exchange(parts, "z")
+    mapped_part = call(
+        map_kernel,
+        shape((factor_inverse.shape[1], width), f32),
+        [VMEM, VMEM, LATER],
         10**9,
-    )(share)
-    parts = exchange(pieces, PLANE)
-    gathered = exchange(copies, "col").reshape(-1, width)
-
-    mapped_part = lax.dot_general(
-        factor_inverse, gathered, (((0,), (0,)), ((), ())), preferred_element_type=f32
-    )
+    )(factor_inverse, gathered, parts)
     mapped_share = lax.psum_scatter(mapped_part, "row", scatter_dimension=0, tiled=True)
-    rows = lax.axis_size("row")
-    mapped = exchange(
-        jnp.broadcast_to(mapped_share[None], (rows,) + mapped_share.shape), "row"
-    ).reshape(-1, width)
-
-    by_plane = call(
-        sum_kernel, jax.ShapeDtypeStruct((planes,) + piece, f32), [VMEM, LATER], 10**7
-    )(parts, copies)
-    by_plane = exchange(by_plane, "z")
-    totals = call(
-        sum_kernel, jax.ShapeDtypeStruct((size,) + piece, f32), [VMEM, LATER], 10**7
-    )(by_plane, mapped_part)
+    totals = call(sum_kernel, shape((size,) + piece, f32), [VMEM, LATER], 10**7)(
+        parts, mapped_part
+    )
     totals = exchange(totals, PLANE)
+    halves = swap(totals)
+
+    copies = call(sum_kernel, shape((rows,) + mapped_share.shape, f32), [VMEM, LATER], 10**7)(
+        mapped_share[None], totals
+    )
+    mapped = exchange(copies, "row").reshape(-1, width)
     rows_total = planes * lax.axis_size("core") * B
     covariance = call(
         functools.partial(inverse_kernel, 1.0 / rows_total),
-        jax.ShapeDtypeStruct(arrow_block.shape, f32),
-        [VMEM, VMEM, LATER],
+        shape(arrow_block.shape, f32),
+        [VMEM, VMEM, VMEM, LATER],
         15 * 10**9,
-    )(totals, arrow_block, mapped_share)
+    )(totals, halves, arrow_block, copies)
     return (mapped, covariance)
 
 
 def solution(mesh):
     tm, row, col = mesh.devices.shape
-    split = Mesh(mesh.devices.reshape(tm // 2, 2, row, col), ("z",) + PLANE)
+    split = Mesh(mesh.devices.reshape(tm // 2, 2, row, col), ("z", "core") + PLANE)
     blocks = P(("z", "core", "col"), None)
     return jax.shard_map(
         per_device,

time: 191 us -> 181 us (0.948)
  blocking collectives: 70.3 us -> 57.2 us
  starting transfers between devices: 14.2 us -> 17.7 us
    all_to_all x2 -> x1, waiting for transfers between devices: 14.3 us -> 0.01 us  [exchange(): return lax.all_to_all(pieces, axes, 0, 0, tiled=True)]
    ppermute x0 -> x2, starting transfers between devices: none -> 13.9 us  [swap(): return lax.ppermute(x, 'core', [(0, 1), (1, 0)])]
    all_to_all x3, blocking collectives: 70.3 us -> 57.2 us  [exchange(): return lax.all_to_all(pieces, axes, 0, 0, tiled=True)]
    reduce_scatter x1, waiting for transfers between devices: 0.01 us -> 11.9 us  [per_device(): lax.psum_scatter(mapped_part, 'row', scatter_dimension=0, tiled=True)]
    all_to_all x2 -> x1, starting transfers between devices: 14.1 us -> 3.67 us  [exchange(): return lax.all_to_all(pieces, axes, 0, 0, tiled=True)]
    broadcast_in_dim x1 -> x0, local copies, waits for them, and re-layouts: 1.93 us -> none  [per_device(): jnp.broadcast_to(mapped_share[None], (rows,) + mapped_share.shape)]
    pallas_call x4 -> x6, Pallas kernels: 14.3 us -> 16.1 us  [the longest x1 13.2 us: per_device(): call(functools.partial(inverse_kernel, 1.0 / rows_total), shape(arrow_blo...]
  transfers between devices with their start and end apart: 4 -> 6, of which waited for: 2 -> 4; matrix products, arithmetic and copies ran while one was open for 1% -> 1% of each run, Pallas kernels for 7% -> 8%
where the time goes in v3:
time: 181 us; the launch traced here: 179 us
  waiting for transfers between devices  66.3 us (37%)
  blocking collectives  57.2 us (32%)
  starting transfers between devices  17.7 us (10%)
  Pallas kernels  16.1 us (9%)
  between operations  13.8 us (8%)
  local copies, waits for them, and re-layouts  4.17 us (2%)
  matrix products  3.1 us (2%)
    all_to_all x3, blocking collectives, exchange(): return lax.all_to_all(pieces, axes, 0, 0, tiled=True)  57.2 us
    reduce_scatter x1, waiting for transfers between devices, per_device(): lax.psum_scatter(jnp.dot(factor_inverse, coupling, preferred_element_type...  53.3 us
    ppermute x2, starting transfers between devices, swap(): return lax.ppermute(x, 'core', [(0, 1), (1, 0)])  13.9 us
    pallas_call x1, Pallas kernels, per_device(): call(functools.partial(inverse_kernel, 1.0 / rows_total), shape(arrow_blo...  13.2 us
    reduce_scatter x1, waiting for transfers between devices, per_device(): lax.psum_scatter(mapped_part, 'row', scatter_dimension=0, tiled=True)  11.9 us
    unnamed x11, local copies, waits for them, and re-layouts  4.17 us
    all_to_all x1, starting transfers between devices, exchange(): return lax.all_to_all(pieces, axes, 0, 0, tiled=True)  3.67 us
  transfers between devices with their start and end apart: 6, of which 4 were waited for; matrix products, arithmetic and copies ran while one was open for 1% of the time, Pallas kernels for 8%

profile of v3, /device:TPU:1, one launch (start us, length us, event | category | flops | bytes accessed | tf_op | source)
XLA Modules:
  0.0 179.3 jit_solution(10654294341624497270)
XLA Ops:
  7.2 0.0 copy-start
  7.2 0.0 reduce-scatter.3.cloned.1.call-start
  7.2 0.9 copy-done
  8.2 3.1 %fusion = f32[1024,384]{1,0:T(8,128)} fusion(bf16[1024,512]{1,0:T(8,128)(2,1)} %factor_ref.1, bf16[512,384]{1,0:T(8,128)(2,1)S(1)} %copy-done), kind=kOutput, calls=%fused_computation | convolution fusion | flops 402653184 | bytes 3014656 | tf_op jit(solution)/shard_map/dot_general | solution.py:159
  11.3 0.0 reduce-scatter.3.cloned.1.call-update
  11.3 0.0 all-gather.2.cloned.1.call-start
  11.3 53.3 %reduce-scatter.3.cloned.1.call-done = f32[128,384]{1,0:T(8,128)} async-done(((f32[1024,384]{1,0:T(8,128)}), f32[128,384]{1,0:T(8,128)}) %reduce-scatter.3.cloned.1.call-update) | async-done | bytes 196624 | tf_op jit(solution)/shard_map/reduce_scatter | solution.py:158
  64.6 0.0 all-gather.2.cloned.1.call-update
  64.6 0.0 reduce-scatter.5.cloned.1.call-start
  64.7 0.9 convert_element_type.3.mine_ref.after_ref
  65.6 0.0 copy-start.1
  65.6 6.2 %collective-permute-start = (bf16[128,384]{1,0:T(8,128)(2,1)S(1)}, bf16[128,384]{1,0:T(8,128)(2,1)S(1)}, u32[]{:S(2)}, u32[]{:S(2)}) collective-permute-start(bf16[128,384]{1,0:T(8,128)(2,1)S(1)} %convert_element_type.3.mine_ref.after_ref), channel_id=1, source_target_pairs={{0,32},{32,0},{1,33},{33,1},{2,34},{34,2},{3,35},{35,3},{4,36},{36... | collective-permute-start | bytes 294920 | tf_op jit(solution)/shard_map/ppermute | solution.py:152
  71.9 0.9 collective-permute-done.other_ref
  72.8 0.2 shard_map.50
  73.0 16.2 %all_to_all.20.parts_ref = f32[32,4,384]{2,1,0:T(4,128)S(1)} all-to-all(f32[32,4,384]{2,1,0:T(4,128)S(1)} %shard_map.50), channel_id=1, replica_groups=mesh['z'=16,'core'=2,'row'=4,'col'=8] {'row','col'}, dimensions={0} | all-to-all | bytes 393216 | tf_op jit(solution)/shard_map/all_to_all | solution.py:148
  89.3 24.4 %all_to_all.21.after_ref.parts_ref = f32[16,4,384]{2,1,0:T(4,128)S(1)} all-to-all(f32[16,4,384]{2,1,0:T(4,128)S(1)} %shard_map.51), channel_id=1, replica_groups=mesh['z'=16,'core'=2,'row'=4,'col'=8] {'z'}, dimensions={0} | all-to-all | bytes 196608 | tf_op jit(solution)/shard_map/all_to_all | solution.py:148
  113.7 0.2 all-gather.2.cloned.1.call-done.sums_ref
  113.8 0.0 copy-done.1
  113.8 0.0 copy-start.3
  113.8 1.4 copy-done.3
  115.3 1.6 shard_map.52.after_ref
  116.9 0.0 reduce-scatter.5.cloned.1.call-update
  116.9 0.0 copy-start.4
  116.9 16.6 %all_to_all.22.after_ref.mine_ref = f32[32,4,384]{2,1,0:T(4,128)S(1)} all-to-all(f32[32,4,384]{2,1,0:T(4,128)S(1)} %shard_map.53), channel_id=1, replica_groups=mesh['z'=16,'core'=2,'row'=4,'col'=8] {'row','col'}, dimensions={0} | all-to-all | bytes 393216 | tf_op jit(solution)/shard_map/all_to_all | solution.py:148
  133.5 7.7 %collective-permute-start.1 = (f32[32,4,384]{2,1,0:T(4,128)S(1)}, f32[32,4,384]{2,1,0:T(4,128)S(1)}, u32[]{:S(2)}, u32[]{:S(2)}) collective-permute-start(f32[32,4,384]{2,1,0:T(4,128)S(1)} %all_to_all.22.after_ref.mine_ref), channel_id=1, source_target_pairs={{0,32},{32,0},{1,33},{33,1},{2,34},{34,2},{3,35},{35,3},{4,36},{36... | collective-permute-start | bytes 589832 | tf_op jit(solution)/shard_map/ppermute | solution.py:152
  141.2 11.9 %reduce-scatter.5.cloned.1.call-done = f32[128,384]{1,0:T(8,128)} async-done(((f32[512,384]{1,0:T(8,128)}), f32[128,384]{1,0:T(8,128)}) %reduce-scatter.5.cloned.1.call-update) | async-done | bytes 196624 | tf_op jit(solution)/shard_map/reduce_scatter | solution.py:182
  153.1 0.0 copy-start.2
  153.1 0.9 copy-done.2
  154.0 0.9 shard_map.54.after_ref
  155.0 3.7 %all-to-all-start.3 = ((f32[4,128,384]{2,1,0:T(8,128)}), f32[4,128,384]{2,1,0:T(8,128)S(1)}, u32[]{:S(2)}, u32[]{:S(2)}) async-start(f32[4,128,384]{2,1,0:T(8,128)} %shard_map.54.after_ref), calls=%async_computation.5 | async-start | bytes 1572864 | tf_op jit(solution)/shard_map/all_to_all | solution.py:148
  158.6 0.0 collective-permute-done.1.other_ref
  158.7 0.0 copy-done.4
  158.7 13.2 %shard_map.55 = f32[384,384]{1,0:T(8,128)} custom-call(f32[32,4,384]{2,1,0:T(4,128)S(1)} %all_to_all.22.after_ref.mine_ref, f32[32,4,384]{2,1,0:T(4,128)S(1)} %collective-permute-done.1.other_ref, f32[384,384]{1,0:T(8,128)S(1)} %copy-done.4, f32[4,128,384]{2,1,0:T(8,128)} %shard_map.54.after_ref), custom_call_target="tpu_custom_call" | custom-call | flops 15000000512 | bytes 1048576 | tf_op jit(solution)/shard_map/pallas_call | solution.py:194
  171.9 0.0 all-to-all-done.3
  171.9 0.9 copy.6
  (2 shorter events, 0.1 us)
Async XLA Ops:
  7.2 1.0 copy-start
  7.2 57.4 %reduce-scatter.3.cloned.1.call-start = ((), (), s32[]{:S(2)}) async-start(), calls=%async_computation.6 | async-start | bytes 1769472 | tf_op jit(solution)/shard_map/reduce_scatter | solution.py:158
  11.3 102.6 %all-gather.2.cloned.1.call-start = ((), (), s32[]{:S(2)}) async-start(), calls=%async_computation.7 | async-start | bytes 1769472 | tf_op jit(solution)/shard_map/all_gather | solution.py:164
  64.6 88.5 %reduce-scatter.5.cloned.1.call-start = ((), (), s32[]{:S(2)}) async-start(), calls=%async_computation.8 | async-start | bytes 983040 | tf_op jit(solution)/shard_map/reduce_scatter | solution.py:182
  65.6 48.2 %copy-start.1 = (bf16[1024,512]{1,0:T(8,128)(2,1)S(1)}, bf16[1024,512]{1,0:T(8,128)(2,1)}, u32[]{:S(2)}) copy-start(bf16[1024,512]{1,0:T(8,128)(2,1)} %factor_ref.1) | copy-start | bytes 3145732
  65.6 7.1 %collective-permute-start = (bf16[128,384]{1,0:T(8,128)(2,1)S(1)}, bf16[128,384]{1,0:T(8,128)(2,1)S(1)}, u32[]{:S(2)}, u32[]{:S(2)}) collective-permute-start(bf16[128,384]{1,0:T(8,128)(2,1)S(1)} %convert_element_type.3.mine_ref.after_ref), channel_id=1, source_target_pairs={{0,32},{32,0},{1,33},{33,1},{2,34},{34,2},{3,35},{35,3},{4,36},{36... | collective-permute-start | bytes 294920 | tf_op jit(solution)/shard_map/ppermute | solution.py:152
  113.8 1.4 copy-start.3
  116.9 41.8 %copy-start.4 = (f32[384,384]{1,0:T(8,128)S(1)}, f32[384,384]{1,0:T(8,128)}, u32[]{:S(2)}) copy-start(f32[384,384]{1,0:T(8,128)} %arrow_ref.1) | copy-start | bytes 1769476
  133.5 25.1 %collective-permute-start.1 = (f32[32,4,384]{2,1,0:T(4,128)S(1)}, f32[32,4,384]{2,1,0:T(4,128)S(1)}, u32[]{:S(2)}, u32[]{:S(2)}) collective-permute-start(f32[32,4,384]{2,1,0:T(4,128)S(1)} %all_to_all.22.after_ref.mine_ref), channel_id=1, source_target_pairs={{0,32},{32,0},{1,33},{33,1},{2,34},{34,2},{3,35},{35,3},{4,36},{36... | collective-permute-start | bytes 589832 | tf_op jit(solution)/shard_map/ppermute | solution.py:152
  153.1 0.9 copy-start.2
  155.0 17.0 %all-to-all-start.3 = ((f32[4,128,384]{2,1,0:T(8,128)}), f32[4,128,384]{2,1,0:T(8,128)S(1)}, u32[]{:S(2)}, u32[]{:S(2)}) async-start(f32[4,128,384]{2,1,0:T(8,128)} %shard_map.54.after_ref), calls=%async_computation.5 | async-start | bytes 1572864 | tf_op jit(solution)/shard_map/all_to_all | solution.py:148
Sparse Core Ops, SparseCore 0:
  11.4 53.1 reduce-scatter.2
  67.3 46.5 all-gather.1
  117.8 35.2 reduce-scatter.4

commit v4 on v3

--- a/solution.py
+++ b/solution.py
@@ -76,23 +76,61 @@
         store(jnp.concatenate([product(1), product(2)], axis=1))
 
 
-def map_kernel(factor_ref, sums_ref, after_ref, out_ref):
-    del after_ref
-    out_ref[...] = lax.dot_general(
-        factor_ref[...],
-        -sums_ref[...].astype(jnp.bfloat16),
-        (((0,), (0,)), ((), ())),
-        preferred_element_type=jnp.float32,
-    )
+def turned(axis, distance):
+    n = lax.axis_size(axis)
+    steps = jnp.where(lax.axis_index("core") == 0, distance % n, -distance % n)
+    return lax.rem(lax.axis_index(axis) + steps, n)
+
+
+def chunk(axis, distance, size):
+    return pl.ds(pl.multiple_of(turned(axis, distance) * size, size), size)
+
+
+def join_kernel(parts_ref, second_ref, first_ref, copies_ref, pair_ref):
+    fan_out(sum_of(parts_ref), copies_ref)
+    n = first_ref.shape[0]
+    pair_ref[:n] = second_ref[...]
+    pair_ref[n:] = first_ref[...]
+
+
+def map_kernel(factor_ref, *refs):
+    *rows_refs, _ = refs[:8]
+    *out_refs, weights_ref = refs[8:]
+    distance = -4
+    n = rows_refs[-1].shape[0]
+    for ref in rows_refs:
+        for i in range(ref.shape[0] // n):
+            weights_ref[chunk("col", distance, n), :] = ref[i * n : (i + 1) * n]
+            distance += 1
+    for distance, out_ref in enumerate(out_refs):
+        out_ref[...] = -lax.dot_general(
+            factor_ref[:, chunk("row", distance, out_ref.shape[0])],
+            weights_ref[...],
+            (((0,), (0,)), ((), ())),
+            preferred_element_type=jnp.float32,
+        )
+
+
+def sum_of(ref):
+    total = ref[0]
+    for i in range(1, ref.shape[0]):
+        total = total + ref[i]
+    return total
+
+
+def fan_out(x, copies_ref):
+    for i in range(copies_ref.shape[0]):
+        copies_ref[i] = x
 
 
 def sum_kernel(parts_ref, after_ref, copies_ref):
     del after_ref
-    total = parts_ref[0]
-    for i in range(1, parts_ref.shape[0]):
-        total = total + parts_ref[i]
-    for i in range(copies_ref.shape[0]):
-        copies_ref[i] = total
+    fan_out(sum_of(parts_ref), copies_ref)
+
+
+def add_kernel(a_ref, b_ref, c_ref, d_ref, after_ref, copies_ref):
+    del after_ref
+    fan_out((a_ref[...] + b_ref[...]) + (c_ref[...] + d_ref[...]), copies_ref)
 
 
 def inverse_kernel(scale, mine_ref, other_ref, arrow_ref, after_ref, out_ref):
@@ -133,12 +171,13 @@
 LATER = pl.BlockSpec(memory_space=pl.ANY)
 
 
-def call(kernel, out_shape, in_specs, flops):
+def call(kernel, out_shape, in_specs, flops, scratch=()):
     return pl.pallas_call(
         kernel,
         out_shape=out_shape,
         in_specs=in_specs,
         out_specs=jax.tree.map(lambda _: VMEM, out_shape),
+        scratch_shapes=scratch,
         compiler_params=pltpu.CompilerParams(vmem_limit_bytes=16 * 2**20),
         cost_estimate=pl.CostEstimate(flops=flops, bytes_accessed=2**20, transcendentals=0),
     )
@@ -148,46 +187,114 @@
     return lax.all_to_all(pieces, axes, 0, 0, tiled=True)
 
 
+def shift(x, axis, distance):
+    n = lax.axis_size(axis)
+    ways = ((0, distance), (n, -distance))
+    return lax.ppermute(
+        x,
+        ("core", axis),
+        [(first + i, first + (i + d) % n) for first, d in ways for i in range(n)],
+    )
+
+
 def swap(x):
     return lax.ppermute(x, "core", [(0, 1), (1, 0)])
+
+
+def far_kernel(factor_ref, coupling_ref, up_ref, down_ref):
+    half, n = up_ref.shape[0], 2 * up_ref.shape[0]
+    far = jnp.dot(
+        factor_ref[chunk("col", 4, n), :], coupling_ref[...], preferred_element_type=jnp.float32
+    )
+    up_ref[...] = far[:half]
+    down_ref[...] = far[half:]
+
+
+def near_kernel(factor_ref, coupling_ref, after_ref, *out_refs):
+    del after_ref
+    for i, out_ref in enumerate(out_refs):
+        out_ref[...] = jnp.dot(
+            factor_ref[chunk("col", i - 3, out_ref.shape[0]), :],
+            coupling_ref[...],
+            preferred_element_type=jnp.float32,
+        )
+
+
+def first_kernel(ahead_ref, behind_ref, up_ref, down_ref, ahead_out, behind_out):
+    half = up_ref.shape[0]
+    ahead_out[:half] = ahead_ref[:half] + up_ref[...]
+    ahead_out[half:] = ahead_ref[half:]
+    behind_out[:half] = behind_ref[:half]
+    behind_out[half:] = behind_ref[half:] + down_ref[...]
+
+
+def step_kernel(ahead_ref, behind_ref, up_ref, down_ref, ahead_out, behind_out):
+    ahead_out[...] = ahead_ref[...] + up_ref[...]
+    behind_out[...] = behind_ref[...] + down_ref[...]
+
+
+def last_kernel(mine_ref, up_ref, down_ref, out_ref):
+    out_ref[...] = (mine_ref[...] + (up_ref[...] + down_ref[...])).astype(out_ref.dtype)
+
+
+def ring_weights(factor_inverse, coupling):
+    shape = jax.ShapeDtypeStruct
+    rows = factor_inverse.shape[0] // lax.axis_size("col")
+    width = coupling.shape[1]
+    full = shape((rows, width), jnp.float32)
+    half = shape((rows // 2, width), jnp.float32)
+    far = call(far_kernel, (half,) * 2, [VMEM] * 2, 10**8)(factor_inverse, coupling)
+    near = call(near_kernel, (full,) * 7, [VMEM, VMEM, LATER], 10**9)(
+        factor_inverse, coupling, far[0]
+    )
+    up, down = far
+    for distance in (3, 2, 1):
+        up, down = shift(up, "col", 1), shift(down, "col", -1)
+        up, down = call(
+            first_kernel if distance == 3 else step_kernel, (full,) * 2, [VMEM] * 4, 10**7
+        )(near[3 + distance], near[3 - distance], up, down)
+    up, down = shift(up, "col", 1), shift(down, "col", -1)
+    return call(last_kernel, shape(full.shape, jnp.bfloat16), [VMEM] * 3, 10**7)(
+        near[3], up, down
+    )
 
 
 def per_device(factor_inverse, coupling, arrow_block):
     f32 = jnp.float32
     shape = jax.ShapeDtypeStruct
-    share = lax.psum_scatter(
-        jnp.dot(factor_inverse, coupling, preferred_element_type=f32),
-        "col",
-        scatter_dimension=0,
-        tiled=True,
-    )
-    gathered = lax.all_gather(share, "col", tiled=True)
-    weights = share.astype(jnp.bfloat16)
-    planes, size, rows = (lax.axis_size(a) for a in ("z", PLANE, "row"))
-    width = share.shape[1]
+    weights = ring_weights(factor_inverse, coupling)
+    planes, size, rows, cols = (lax.axis_size(a) for a in ("z", PLANE, "row", "col"))
+    height, width = weights.shape
     piece = (width // 3 // size, width)
 
-    pieces = call(gram_kernel, shape((size,) + piece, f32), [VMEM] * 2, 10**9)(
-        weights, swap(weights)
-    )
+    other = swap(weights)
+    near = {d: shift(weights, "col", -d) for d in (-1, 1, -2, 2)}
+    pieces = call(gram_kernel, shape((size,) + piece, f32), [VMEM] * 2, 10**9)(weights, other)
     parts = exchange(pieces, PLANE)
-    parts = call(sum_kernel, shape((planes,) + piece, f32), [VMEM, LATER], 10**7)(parts, weights)
+    parts, pair = call(
+        join_kernel,
+        (shape((planes,) + piece, f32), shape((2 * height, width), weights.dtype)),
+        [VMEM] * 3,
+        10**7,
+    )(parts, near[-2], near[-1])
+    far = shift(pair, "col", 2), shift(near[1], "col", -2)
     parts = exchange(parts, "z")
-    mapped_part = call(
+    block = shape((factor_inverse.shape[1] // rows, width), f32)
+    mapped = call(
         map_kernel,
-        shape((factor_inverse.shape[1], width), f32),
-        [VMEM, VMEM, LATER],
+        (block,) * rows,
+        [VMEM] * 8 + [LATER],
         10**9,
-    )(factor_inverse, gathered, parts)
-    mapped_share = lax.psum_scatter(mapped_part, "row", scatter_dimension=0, tiled=True)
+        [pltpu.VMEM((cols * height, width), weights.dtype)],
+    )(factor_inverse, far[0], near[-2], near[-1], weights, near[1], near[2], far[1], parts)
+    arrived = [shift(mapped[d], "row", d) for d in range(1, rows)]
     totals = call(sum_kernel, shape((size,) + piece, f32), [VMEM, LATER], 10**7)(
-        parts, mapped_part
+        parts, mapped[0]
     )
     totals = exchange(totals, PLANE)
     halves = swap(totals)
-
-    copies = call(sum_kernel, shape((rows,) + mapped_share.shape, f32), [VMEM, LATER], 10**7)(
-        mapped_share[None], totals
+    copies = call(add_kernel, shape((rows,) + block.shape, f32), [VMEM] * 4 + [LATER], 10**7)(
+        mapped[0], *arrived, totals
     )
     mapped = exchange(copies, "row").reshape(-1, width)
     rows_total = planes * lax.axis_size("core") * B

time: 181 us -> 159 us (0.88)
  starting transfers between devices: 17.7 us -> 103 us
  blocking collectives: 57.2 us -> 0 us
  waiting for transfers between devices: 66.3 us -> 33.3 us
  between operations: 13.8 us -> 0.93 us
  matrix products: 3.1 us -> 0 us
  Pallas kernels: 16.1 us -> 18.3 us
    reduce_scatter x2 -> x0, waiting for transfers between devices: 65.2 us -> none  [the longest x1 53.3 us: per_device(): lax.psum_scatter(jnp.dot(factor_inverse, coupling, preferred_element_type...]
    all_to_all x3 -> x0, blocking collectives: 57.2 us -> none  [exchange(): return lax.all_to_all(pieces, axes, 0, 0, tiled=True)]
    ppermute x0 -> x17, starting transfers between devices: none -> 55.1 us  [shift(): lax.ppermute(x, ('core', axis), [(first + i, first + (i + d) % n) for fir...]
    ppermute x0 -> x17, waiting for transfers between devices: none -> 32.3 us  [shift(): lax.ppermute(x, ('core', axis), [(first + i, first + (i + d) % n) for fir...]
    all_to_all x1 -> x4, starting transfers between devices: 3.67 us -> 29.2 us  [exchange(): return lax.all_to_all(pieces, axes, 0, 0, tiled=True)]
    ppermute x2, starting transfers between devices: 13.9 us -> 18.6 us  [swap(): return lax.ppermute(x, 'core', [(0, 1), (1, 0)])]
    dot_general x1 -> x0, matrix products: 3.1 us -> none  [per_device(): jnp.dot(factor_inverse, coupling, preferred_element_type=f32)]
    unnamed x11 -> x9, local copies, waits for them, and re-layouts: 4.17 us -> 3.11 us
  transfers between devices with their start and end apart: 6 -> 23, of which waited for: 4 -> 12; matrix products, arithmetic and copies ran while one was open for 1% -> 0% of each run, Pallas kernels for 8% -> 9%
where the time goes in v4:
time: 159 us; the launch traced here: 158 us
  starting transfers between devices  103 us (65%)
  waiting for transfers between devices  33.3 us (21%)
  Pallas kernels  18.3 us (12%)
  local copies, waits for them, and re-layouts  3.11 us (2%)
    ppermute x17, starting transfers between devices, shift(): lax.ppermute(x, ('core', axis), [(first + i, first + (i + d) % n) for fir...  55.1 us
    ppermute x17, waiting for transfers between devices, shift(): lax.ppermute(x, ('core', axis), [(first + i, first + (i + d) % n) for fir...  32.3 us
    all_to_all x4, starting transfers between devices, exchange(): return lax.all_to_all(pieces, axes, 0, 0, tiled=True)  29.2 us
    ppermute x2, starting transfers between devices, swap(): return lax.ppermute(x, 'core', [(0, 1), (1, 0)])  18.6 us
    pallas_call x1, Pallas kernels, per_device(): call(functools.partial(inverse_kernel, 1.0 / rows_total), shape(arrow_blo...  13.2 us
  transfers between devices with their start and end apart: 23, of which 12 were waited for; matrix products, arithmetic and copies ran while one was open for 0% of the time, Pallas kernels for 9%

profile of v4, /device:TPU:1, one launch (start us, length us, event | category | flops | bytes accessed | tf_op | source)
XLA Modules:
  0.0 158.5 jit_solution(17895059808549332514)
XLA Ops:
  0.6 0.0 copy-start
  0.6 1.2 copy-done
  1.9 0.0 copy-start.2
  1.9 1.0 copy-done.2
  2.9 0.2 shard_map.50
  3.1 5.9 %collective-permute-start = (f32[64,384]{1,0:T(8,128)S(1)}, f32[64,384]{1,0:T(8,128)S(1)}, u32[]{:S(2)}, u32[]{:S(2)}) collective-permute-start(f32[64,384]{1,0:T(8,128)S(1)} %get-tuple-element.23.after_ref), channel_id=1, source_target_pairs={{0,1},{1,2},{2,3},{3,4},{4,5},{5,6},{6,7},{7,0},{32,39},{33,32},{3... | collective-permute-start | bytes 294920 | tf_op jit(solution)/shard_map/ppermute | solution.py:193
  9.0 1.9 %collective-permute-start.1 = (f32[64,384]{1,0:T(8,128)S(1)}, f32[64,384]{1,0:T(8,128)S(1)}, u32[]{:S(2)}, u32[]{:S(2)}) collective-permute-start(f32[64,384]{1,0:T(8,128)S(1)} %get-tuple-element.31), channel_id=1, source_target_pairs={{0,7},{1,0},{2,1},{3,2},{4,3},{5,4},{6,5},{7,6},{32,33},{33,34},{3... | collective-permute-start | bytes 294920 | tf_op jit(solution)/shard_map/ppermute | solution.py:193
  10.9 0.6 shard_map.51
  11.6 0.0 collective-permute-done.up_ref
  11.6 4.0 %collective-permute-done.1.down_ref = f32[64,384]{1,0:T(8,128)S(1)} collective-permute-done((f32[64,384]{1,0:T(8,128)S(1)}, f32[64,384]{1,0:T(8,128)S(1)}, u32[]{:S(2)}, u32[]{:S(2)}) %collective-permute-start.1) | collective-permute-done | bytes 98336 | tf_op jit(solution)/shard_map/ppermute | solution.py:193
  15.6 1.9 %collective-permute-start.2 = (f32[128,384]{1,0:T(8,128)S(1)}, f32[128,384]{1,0:T(8,128)S(1)}, u32[]{:S(2)}, u32[]{:S(2)}) collective-permute-start(f32[128,384]{1,0:T(8,128)S(1)} %get-tuple-element.32), channel_id=1, source_target_pairs={{0,1},{1,2},{2,3},{3,4},{4,5},{5,6},{6,7},{7,0},{32,39},{33,32},{3... | collective-permute-start | bytes 589832 | tf_op jit(solution)/shard_map/ppermute | solution.py:193
  17.6 3.4 %collective-permute-start.3 = (f32[128,384]{1,0:T(8,128)S(1)}, f32[128,384]{1,0:T(8,128)S(1)}, u32[]{:S(2)}, u32[]{:S(2)}) collective-permute-start(f32[128,384]{1,0:T(8,128)S(1)} %get-tuple-element.33), channel_id=1, source_target_pairs={{0,7},{1,0},{2,1},{3,2},{4,3},{5,4},{6,5},{7,6},{32,33},{33,34},{3... | collective-permute-start | bytes 589832 | tf_op jit(solution)/shard_map/ppermute | solution.py:193
  20.9 1.1 collective-permute-done.2.up_ref
  22.0 4.2 %collective-permute-done.3.down_ref = f32[128,384]{1,0:T(8,128)S(1)} collective-permute-done((f32[128,384]{1,0:T(8,128)S(1)}, f32[128,384]{1,0:T(8,128)S(1)}, u32[]{:S(2)}, u32[]{:S(2)}) %collective-permute-start.3) | collective-permute-done | bytes 196640 | tf_op jit(solution)/shard_map/ppermute | solution.py:193
  26.3 1.9 %collective-permute-start.4 = (f32[128,384]{1,0:T(8,128)S(1)}, f32[128,384]{1,0:T(8,128)S(1)}, u32[]{:S(2)}, u32[]{:S(2)}) collective-permute-start(f32[128,384]{1,0:T(8,128)S(1)} %get-tuple-element.34), channel_id=1, source_target_pairs={{0,1},{1,2},{2,3},{3,4},{4,5},{5,6},{6,7},{7,0},{32,39},{33,32},{3... | collective-permute-start | bytes 589832 | tf_op jit(solution)/shard_map/ppermute | solution.py:193
  28.2 3.4 %collective-permute-start.5 = (f32[128,384]{1,0:T(8,128)S(1)}, f32[128,384]{1,0:T(8,128)S(1)}, u32[]{:S(2)}, u32[]{:S(2)}) collective-permute-start(f32[128,384]{1,0:T(8,128)S(1)} %get-tuple-element.35), channel_id=1, source_target_pairs={{0,7},{1,0},{2,1},{3,2},{4,3},{5,4},{6,5},{7,6},{32,33},{33,34},{3... | collective-permute-start | bytes 589832 | tf_op jit(solution)/shard_map/ppermute | solution.py:193
  31.6 1.1 collective-permute-done.4.up_ref
  32.7 4.4 %collective-permute-done.5.down_ref = f32[128,384]{1,0:T(8,128)S(1)} collective-permute-done((f32[128,384]{1,0:T(8,128)S(1)}, f32[128,384]{1,0:T(8,128)S(1)}, u32[]{:S(2)}, u32[]{:S(2)}) %collective-permute-start.5) | collective-permute-done | bytes 196640 | tf_op jit(solution)/shard_map/ppermute | solution.py:193
  37.2 1.9 %collective-permute-start.6 = (f32[128,384]{1,0:T(8,128)S(1)}, f32[128,384]{1,0:T(8,128)S(1)}, u32[]{:S(2)}, u32[]{:S(2)}) collective-permute-start(f32[128,384]{1,0:T(8,128)S(1)} %get-tuple-element.36), channel_id=1, source_target_pairs={{0,1},{1,2},{2,3},{3,4},{4,5},{5,6},{6,7},{7,0},{32,39},{33,32},{3... | collective-permute-start | bytes 589832 | tf_op jit(solution)/shard_map/ppermute | solution.py:193
  39.1 3.4 %collective-permute-start.7 = (f32[128,384]{1,0:T(8,128)S(1)}, f32[128,384]{1,0:T(8,128)S(1)}, u32[]{:S(2)}, u32[]{:S(2)}) collective-permute-start(f32[128,384]{1,0:T(8,128)S(1)} %get-tuple-element.37), channel_id=1, source_target_pairs={{0,7},{1,0},{2,1},{3,2},{4,3},{5,4},{6,5},{7,6},{32,33},{33,34},{3... | collective-permute-start | bytes 589832 | tf_op jit(solution)/shard_map/ppermute | solution.py:193
  42.5 1.1 collective-permute-done.6.up_ref
  43.6 4.3 %collective-permute-done.7.down_ref = f32[128,384]{1,0:T(8,128)S(1)} collective-permute-done((f32[128,384]{1,0:T(8,128)S(1)}, f32[128,384]{1,0:T(8,128)S(1)}, u32[]{:S(2)}, u32[]{:S(2)}) %collective-permute-start.7) | collective-permute-done | bytes 196640 | tf_op jit(solution)/shard_map/ppermute | solution.py:193
  47.9 0.0 copy-start.1
  47.9 12.8 %collective-permute-start.8 = (bf16[128,384]{1,0:T(8,128)(2,1)S(1)}, bf16[128,384]{1,0:T(8,128)(2,1)S(1)}, u32[]{:S(2)}, u32[]{:S(2)}) collective-permute-start(bf16[128,384]{1,0:T(8,128)(2,1)S(1)} %shard_map.55.mine_ref.refs_3_), channel_id=1, source_target_pairs={{0,32},{32,0},{1,33},{33,1},{2,34},{34,2},{3,35},{35,3},{4,36},{36... | collective-permute-start | bytes 294920 | tf_op jit(solution)/shard_map/ppermute | solution.py:201
  60.7 0.9 collective-permute-done.8.other_ref
  61.7 0.9 shard_map.56
  62.6 5.8 %all-to-all-start = ((f32[32,4,384]{2,1,0:T(4,128)}), f32[32,4,384]{2,1,0:T(4,128)S(1)}, u32[]{:S(2)}, u32[]{:S(2)}) async-start(f32[32,4,384]{2,1,0:T(4,128)} %shard_map.56), calls=%async_computation | async-start | bytes 393216 | tf_op jit(solution)/shard_map/all_to_all | solution.py:187
  68.4 4.4 %collective-permute-start.10 = (bf16[128,384]{1,0:T(8,128)(2,1)S(1)}, bf16[128,384]{1,0:T(8,128)(2,1)S(1)}, u32[]{:S(2)}, u32[]{:S(2)}) collective-permute-start(bf16[128,384]{1,0:T(8,128)(2,1)S(1)} %shard_map.55.mine_ref.refs_3_), channel_id=1, source_target_pairs={{0,1},{1,2},{2,3},{3,4},{4,5},{5,6},{6,7},{7,0},{32,39},{33,32},{3... | collective-permute-start | bytes 294920 | tf_op jit(solution)/shard_map/ppermute | solution.py:193
  72.7 4.0 %collective-permute-start.9 = (bf16[128,384]{1,0:T(8,128)(2,1)S(1)}, bf16[128,384]{1,0:T(8,128)(2,1)S(1)}, u32[]{:S(2)}, u32[]{:S(2)}) collective-permute-start(bf16[128,384]{1,0:T(8,128)(2,1)S(1)} %shard_map.55.mine_ref.refs_3_), channel_id=1, source_target_pairs={{0,2},{1,3},{2,4},{3,5},{4,6},{5,7},{6,0},{7,1},{32,38},{33,39},{3... | collective-permute-start | bytes 294920 | tf_op jit(solution)/shard_map/ppermute | solution.py:193
  76.7 0.0 collective-permute-done.10.first_ref.refs_2_
  76.8 3.2 %collective-permute-done.9.second_ref.refs_1_ = bf16[128,384]{1,0:T(8,128)(2,1)S(1)} collective-permute-done((bf16[128,384]{1,0:T(8,128)(2,1)S(1)}, bf16[128,384]{1,0:T(8,128)(2,1)S(1)}, u32[]{:S(2)}, u32[]{:S(2)}) %collective-permute-start.9) | collective-permute-done | bytes 98336 | tf_op jit(solution)/shard_map/ppermute | solution.py:193
  80.0 0.0 all-to-all-done.parts_ref
  80.0 0.7 shard_map.57
  80.7 10.9 %all-to-all-start.1 = ((f32[16,4,384]{2,1,0:T(4,128)}), f32[16,4,384]{2,1,0:T(4,128)S(1)}, u32[]{:S(2)}, u32[]{:S(2)}) async-start(f32[16,4,384]{2,1,0:T(4,128)} %get-tuple-element.39), calls=%async_computation.1 | async-start | bytes 196608 | tf_op jit(solution)/shard_map/all_to_all | solution.py:187
  91.6 2.3 %collective-permute-start.12 = (bf16[128,384]{1,0:T(8,128)(2,1)S(1)}, bf16[128,384]{1,0:T(8,128)(2,1)S(1)}, u32[]{:S(2)}, u32[]{:S(2)}) collective-permute-start(bf16[128,384]{1,0:T(8,128)(2,1)S(1)} %shard_map.55.mine_ref.refs_3_), channel_id=1, source_target_pairs={{0,7},{1,0},{2,1},{3,2},{4,3},{5,4},{6,5},{7,6},{32,33},{33,34},{3... | collective-permute-start | bytes 294920 | tf_op jit(solution)/shard_map/ppermute | solution.py:193
  93.9 5.1 %collective-permute-start.11 = (bf16[256,384]{1,0:T(8,128)(2,1)S(1)}, bf16[256,384]{1,0:T(8,128)(2,1)S(1)}, u32[]{:S(2)}, u32[]{:S(2)}) collective-permute-start(bf16[256,384]{1,0:T(8,128)(2,1)S(1)} %get-tuple-element.38), channel_id=1, source_target_pairs={{0,2},{1,3},{2,4},{3,5},{4,6},{5,7},{6,0},{7,1},{32,38},{33,39},{3... | collective-permute-start | bytes 589832 | tf_op jit(solution)/shard_map/ppermute | solution.py:193
  99.1 1.9 %collective-permute-start.13 = (bf16[128,384]{1,0:T(8,128)(2,1)S(1)}, bf16[128,384]{1,0:T(8,128)(2,1)S(1)}, u32[]{:S(2)}, u32[]{:S(2)}) collective-permute-start(bf16[128,384]{1,0:T(8,128)(2,1)S(1)} %shard_map.55.mine_ref.refs_3_), channel_id=1, source_target_pairs={{0,6},{1,7},{2,0},{3,1},{4,2},{5,3},{6,4},{7,5},{32,34},{33,35},{3... | collective-permute-start | bytes 294920 | tf_op jit(solution)/shard_map/ppermute | solution.py:193
  101.0 0.0 collective-permute-done.12.refs_4_
  101.0 4.3 %collective-permute-start.14 = (bf16[128,384]{1,0:T(8,128)(2,1)S(1)}, bf16[128,384]{1,0:T(8,128)(2,1)S(1)}, u32[]{:S(2)}, u32[]{:S(2)}) collective-permute-start(bf16[128,384]{1,0:T(8,128)(2,1)S(1)} %collective-permute-done.12.refs_4_), channel_id=1, source_target_pairs={{0,6},{1,7},{2,0},{3,1},{4,2},{5,3},{6,4},{7,5},{32,34},{33,35},{3... | collective-permute-start | bytes 294920 | tf_op jit(solution)/shard_map/ppermute | solution.py:193
  105.3 1.4 collective-permute-done.13.refs_5_
  106.7 4.8 %collective-permute-done.14.refs_6_ = bf16[128,384]{1,0:T(8,128)(2,1)S(1)} collective-permute-done((bf16[128,384]{1,0:T(8,128)(2,1)S(1)}, bf16[128,384]{1,0:T(8,128)(2,1)S(1)}, u32[]{:S(2)}, u32[]{:S(2)}) %collective-permute-start.14) | collective-permute-done | bytes 98336 | tf_op jit(solution)/shard_map/ppermute | solution.py:193
  111.5 0.0 collective-permute-done.11.refs_0_
  111.5 0.0 all-to-all-done.1.refs_7_.parts_ref
  111.5 0.0 copy-done.1
  111.5 0.8 shard_map.58
  112.4 0.7 shard_map.59
  113.1 8.7 %all-to-all-start.2 = ((f32[32,4,384]{2,1,0:T(4,128)}), f32[32,4,384]{2,1,0:T(4,128)S(1)}, u32[]{:S(2)}, u32[]{:S(2)}) async-start(f32[32,4,384]{2,1,0:T(4,128)} %shard_map.59), calls=%async_computation.2 | async-start | bytes 393216 | tf_op jit(solution)/shard_map/all_to_all | solution.py:187
  121.8 4.4 %collective-permute-start.15 = (f32[128,384]{1,0:T(8,128)S(1)}, f32[128,384]{1,0:T(8,128)S(1)}, u32[]{:S(2)}, u32[]{:S(2)}) collective-permute-start(f32[128,384]{1,0:T(8,128)S(1)} %get-tuple-element.41), channel_id=1, source_target_pairs={{0,8},{8,16},{16,24},{24,0},{32,56},{40,32},{48,40},{56,48},{1,9},... | collective-permute-start | bytes 589832 | tf_op jit(solution)/shard_map/ppermute | solution.py:193
  126.2 2.4 %collective-permute-start.16 = (f32[128,384]{1,0:T(8,128)S(1)}, f32[128,384]{1,0:T(8,128)S(1)}, u32[]{:S(2)}, u32[]{:S(2)}) collective-permute-start(f32[128,384]{1,0:T(8,128)S(1)} %get-tuple-element.42), channel_id=1, source_target_pairs={{0,16},{8,24},{16,0},{24,8},{32,48},{40,56},{48,32},{56,40},{1,17}... | collective-permute-start | bytes 589832 | tf_op jit(solution)/shard_map/ppermute | solution.py:193
  128.6 2.5 %collective-permute-start.17 = (f32[128,384]{1,0:T(8,128)S(1)}, f32[128,384]{1,0:T(8,128)S(1)}, u32[]{:S(2)}, u32[]{:S(2)}) collective-permute-start(f32[128,384]{1,0:T(8,128)S(1)} %get-tuple-element.43), channel_id=1, source_target_pairs={{0,24},{8,0},{16,8},{24,16},{32,40},{40,48},{48,56},{56,32},{1,25}... | collective-permute-start | bytes 589832 | tf_op jit(solution)/shard_map/ppermute | solution.py:193
  131.1 0.0 all-to-all-done.2.after_ref.mine_ref
  131.2 5.7 %collective-permute-start.18 = (f32[32,4,384]{2,1,0:T(4,128)S(1)}, f32[32,4,384]{2,1,0:T(4,128)S(1)}, u32[]{:S(2)}, u32[]{:S(2)}) collective-permute-start(f32[32,4,384]{2,1,0:T(4,128)S(1)} %all-to-all-done.2.after_ref.mine_ref), channel_id=1, source_target_pairs={{0,32},{32,0},{1,33},{33,1},{2,34},{34,2},{3,35},{35,3},{4,36},{36... | collective-permute-start | bytes 589832 | tf_op jit(solution)/shard_map/ppermute | solution.py:201
  136.9 0.0 collective-permute-done.15.b_ref
  136.9 0.0 collective-permute-done.16.c_ref
  136.9 2.6 %collective-permute-done.17.d_ref = f32[128,384]{1,0:T(8,128)S(1)} collective-permute-done((f32[128,384]{1,0:T(8,128)S(1)}, f32[128,384]{1,0:T(8,128)S(1)}, u32[]{:S(2)}, u32[]{:S(2)}) %collective-permute-start.17) | collective-permute-done | bytes 196640 | tf_op jit(solution)/shard_map/ppermute | solution.py:193
  139.6 0.9 shard_map.60.after_ref
  140.5 0.0 copy-start.3
  140.5 3.8 %all-to-all-start.3 = ((f32[4,128,384]{2,1,0:T(8,128)}), f32[4,128,384]{2,1,0:T(8,128)S(1)}, u32[]{:S(2)}, u32[]{:S(2)}) async-start(f32[4,128,384]{2,1,0:T(8,128)} %shard_map.60.after_ref), calls=%async_computation.3 | async-start | bytes 1572864 | tf_op jit(solution)/shard_map/all_to_all | solution.py:187
  144.3 0.0 collective-permute-done.18.other_ref
  144.3 0.0 copy-done.3
  144.3 13.2 %shard_map.61 = f32[384,384]{1,0:T(8,128)} custom-call(f32[32,4,384]{2,1,0:T(4,128)S(1)} %all-to-all-done.2.after_ref.mine_ref, f32[32,4,384]{2,1,0:T(4,128)S(1)} %collective-permute-done.18.other_ref, f32[384,384]{1,0:T(8,128)S(1)} %copy-done.3, f32[4,128,384]{2,1,0:T(8,128)} %shard_map.60.after_ref), custom_call_target="tpu_custom_call" | custom-call | flops 15000000512 | bytes 1048576 | tf_op jit(solution)/shard_map/pallas_call | solution.py:301
  157.6 0.0 all-to-all-done.3
  157.6 0.9 copy.6
  (4 shorter events, 0.1 us)
Async XLA Ops:
  0.6 1.2 copy-start
  1.9 1.0 copy-start.2
  3.1 8.5 %collective-permute-start = (f32[64,384]{1,0:T(8,128)S(1)}, f32[64,384]{1,0:T(8,128)S(1)}, u32[]{:S(2)}, u32[]{:S(2)}) collective-permute-start(f32[64,384]{1,0:T(8,128)S(1)} %get-tuple-element.23.after_ref), channel_id=1, source_target_pairs={{0,1},{1,2},{2,3},{3,4},{4,5},{5,6},{6,7},{7,0},{32,39},{33,32},{3... | collective-permute-start | bytes 294920 | tf_op jit(solution)/shard_map/ppermute | solution.py:193
  9.0 6.6 %collective-permute-start.1 = (f32[64,384]{1,0:T(8,128)S(1)}, f32[64,384]{1,0:T(8,128)S(1)}, u32[]{:S(2)}, u32[]{:S(2)}) collective-permute-start(f32[64,384]{1,0:T(8,128)S(1)} %get-tuple-element.31), channel_id=1, source_target_pairs={{0,7},{1,0},{2,1},{3,2},{4,3},{5,4},{6,5},{7,6},{32,33},{33,34},{3... | collective-permute-start | bytes 294920 | tf_op jit(solution)/shard_map/ppermute | solution.py:193
  15.6 6.4 %collective-permute-start.2 = (f32[128,384]{1,0:T(8,128)S(1)}, f32[128,384]{1,0:T(8,128)S(1)}, u32[]{:S(2)}, u32[]{:S(2)}) collective-permute-start(f32[128,384]{1,0:T(8,128)S(1)} %get-tuple-element.32), channel_id=1, source_target_pairs={{0,1},{1,2},{2,3},{3,4},{4,5},{5,6},{6,7},{7,0},{32,39},{33,32},{3... | collective-permute-start | bytes 589832 | tf_op jit(solution)/shard_map/ppermute | solution.py:193
  17.6 8.7 %collective-permute-start.3 = (f32[128,384]{1,0:T(8,128)S(1)}, f32[128,384]{1,0:T(8,128)S(1)}, u32[]{:S(2)}, u32[]{:S(2)}) collective-permute-start(f32[128,384]{1,0:T(8,128)S(1)} %get-tuple-element.33), channel_id=1, source_target_pairs={{0,7},{1,0},{2,1},{3,2},{4,3},{5,4},{6,5},{7,6},{32,33},{33,34},{3... | collective-permute-start | bytes 589832 | tf_op jit(solution)/shard_map/ppermute | solution.py:193
  26.3 6.4 %collective-permute-start.4 = (f32[128,384]{1,0:T(8,128)S(1)}, f32[128,384]{1,0:T(8,128)S(1)}, u32[]{:S(2)}, u32[]{:S(2)}) collective-permute-start(f32[128,384]{1,0:T(8,128)S(1)} %get-tuple-element.34), channel_id=1, source_target_pairs={{0,1},{1,2},{2,3},{3,4},{4,5},{5,6},{6,7},{7,0},{32,39},{33,32},{3... | collective-permute-start | bytes 589832 | tf_op jit(solution)/shard_map/ppermute | solution.py:193
  28.2 8.9 %collective-permute-start.5 = (f32[128,384]{1,0:T(8,128)S(1)}, f32[128,384]{1,0:T(8,128)S(1)}, u32[]{:S(2)}, u32[]{:S(2)}) collective-permute-start(f32[128,384]{1,0:T(8,128)S(1)} %get-tuple-element.35), channel_id=1, source_target_pairs={{0,7},{1,0},{2,1},{3,2},{4,3},{5,4},{6,5},{7,6},{32,33},{33,34},{3... | collective-permute-start | bytes 589832 | tf_op jit(solution)/shard_map/ppermute | solution.py:193
  37.2 6.4 %collective-permute-start.6 = (f32[128,384]{1,0:T(8,128)S(1)}, f32[128,384]{1,0:T(8,128)S(1)}, u32[]{:S(2)}, u32[]{:S(2)}) collective-permute-start(f32[128,384]{1,0:T(8,128)S(1)} %get-tuple-element.36), channel_id=1, source_target_pairs={{0,1},{1,2},{2,3},{3,4},{4,5},{5,6},{6,7},{7,0},{32,39},{33,32},{3... | collective-permute-start | bytes 589832 | tf_op jit(solution)/shard_map/ppermute | solution.py:193
  39.1 8.8 %collective-permute-start.7 = (f32[128,384]{1,0:T(8,128)S(1)}, f32[128,384]{1,0:T(8,128)S(1)}, u32[]{:S(2)}, u32[]{:S(2)}) collective-permute-start(f32[128,384]{1,0:T(8,128)S(1)} %get-tuple-element.37), channel_id=1, source_target_pairs={{0,7},{1,0},{2,1},{3,2},{4,3},{5,4},{6,5},{7,6},{32,33},{33,34},{3... | collective-permute-start | bytes 589832 | tf_op jit(solution)/shard_map/ppermute | solution.py:193
  47.9 63.6 %copy-start.1 = (bf16[1024,512]{1,0:T(8,128)(2,1)S(1)}, bf16[1024,512]{1,0:T(8,128)(2,1)}, u32[]{:S(2)}) copy-start(bf16[1024,512]{1,0:T(8,128)(2,1)} %factor_ref.5) | copy-start | bytes 3145732
  47.9 13.8 %collective-permute-start.8 = (bf16[128,384]{1,0:T(8,128)(2,1)S(1)}, bf16[128,384]{1,0:T(8,128)(2,1)S(1)}, u32[]{:S(2)}, u32[]{:S(2)}) collective-permute-start(bf16[128,384]{1,0:T(8,128)(2,1)S(1)} %shard_map.55.mine_ref.refs_3_), channel_id=1, source_target_pairs={{0,32},{32,0},{1,33},{33,1},{2,34},{34,2},{3,35},{35,3},{4,36},{36... | collective-permute-start | bytes 294920 | tf_op jit(solution)/shard_map/ppermute | solution.py:201
  62.6 17.4 %all-to-all-start = ((f32[32,4,384]{2,1,0:T(4,128)}), f32[32,4,384]{2,1,0:T(4,128)S(1)}, u32[]{:S(2)}, u32[]{:S(2)}) async-start(f32[32,4,384]{2,1,0:T(4,128)} %shard_map.56), calls=%async_computation | async-start | bytes 393216 | tf_op jit(solution)/shard_map/all_to_all | solution.py:187
  68.4 8.4 %collective-permute-start.10 = (bf16[128,384]{1,0:T(8,128)(2,1)S(1)}, bf16[128,384]{1,0:T(8,128)(2,1)S(1)}, u32[]{:S(2)}, u32[]{:S(2)}) collective-permute-start(bf16[128,384]{1,0:T(8,128)(2,1)S(1)} %shard_map.55.mine_ref.refs_3_), channel_id=1, source_target_pairs={{0,1},{1,2},{2,3},{3,4},{4,5},{5,6},{6,7},{7,0},{32,39},{33,32},{3... | collective-permute-start | bytes 294920 | tf_op jit(solution)/shard_map/ppermute | solution.py:193
  72.7 7.2 %collective-permute-start.9 = (bf16[128,384]{1,0:T(8,128)(2,1)S(1)}, bf16[128,384]{1,0:T(8,128)(2,1)S(1)}, u32[]{:S(2)}, u32[]{:S(2)}) collective-permute-start(bf16[128,384]{1,0:T(8,128)(2,1)S(1)} %shard_map.55.mine_ref.refs_3_), channel_id=1, source_target_pairs={{0,2},{1,3},{2,4},{3,5},{4,6},{5,7},{6,0},{7,1},{32,38},{33,39},{3... | collective-permute-start | bytes 294920 | tf_op jit(solution)/shard_map/ppermute | solution.py:193
  80.7 30.9 %all-to-all-start.1 = ((f32[16,4,384]{2,1,0:T(4,128)}), f32[16,4,384]{2,1,0:T(4,128)S(1)}, u32[]{:S(2)}, u32[]{:S(2)}) async-start(f32[16,4,384]{2,1,0:T(4,128)} %get-tuple-element.39), calls=%async_computation.1 | async-start | bytes 196608 | tf_op jit(solution)/shard_map/all_to_all | solution.py:187
  91.6 9.4 %collective-permute-start.12 = (bf16[128,384]{1,0:T(8,128)(2,1)S(1)}, bf16[128,384]{1,0:T(8,128)(2,1)S(1)}, u32[]{:S(2)}, u32[]{:S(2)}) collective-permute-start(bf16[128,384]{1,0:T(8,128)(2,1)S(1)} %shard_map.55.mine_ref.refs_3_), channel_id=1, source_target_pairs={{0,7},{1,0},{2,1},{3,2},{4,3},{5,4},{6,5},{7,6},{32,33},{33,34},{3... | collective-permute-start | bytes 294920 | tf_op jit(solution)/shard_map/ppermute | solution.py:193
  93.9 17.6 %collective-permute-start.11 = (bf16[256,384]{1,0:T(8,128)(2,1)S(1)}, bf16[256,384]{1,0:T(8,128)(2,1)S(1)}, u32[]{:S(2)}, u32[]{:S(2)}) collective-permute-start(bf16[256,384]{1,0:T(8,128)(2,1)S(1)} %get-tuple-element.38), channel_id=1, source_target_pairs={{0,2},{1,3},{2,4},{3,5},{4,6},{5,7},{6,0},{7,1},{32,38},{33,39},{3... | collective-permute-start | bytes 589832 | tf_op jit(solution)/shard_map/ppermute | solution.py:193
  99.1 7.6 %collective-permute-start.13 = (bf16[128,384]{1,0:T(8,128)(2,1)S(1)}, bf16[128,384]{1,0:T(8,128)(2,1)S(1)}, u32[]{:S(2)}, u32[]{:S(2)}) collective-permute-start(bf16[128,384]{1,0:T(8,128)(2,1)S(1)} %shard_map.55.mine_ref.refs_3_), channel_id=1, source_target_pairs={{0,6},{1,7},{2,0},{3,1},{4,2},{5,3},{6,4},{7,5},{32,34},{33,35},{3... | collective-permute-start | bytes 294920 | tf_op jit(solution)/shard_map/ppermute | solution.py:193
  101.0 10.5 %collective-permute-start.14 = (bf16[128,384]{1,0:T(8,128)(2,1)S(1)}, bf16[128,384]{1,0:T(8,128)(2,1)S(1)}, u32[]{:S(2)}, u32[]{:S(2)}) collective-permute-start(bf16[128,384]{1,0:T(8,128)(2,1)S(1)} %collective-permute-done.12.refs_4_), channel_id=1, source_target_pairs={{0,6},{1,7},{2,0},{3,1},{4,2},{5,3},{6,4},{7,5},{32,34},{33,35},{3... | collective-permute-start | bytes 294920 | tf_op jit(solution)/shard_map/ppermute | solution.py:193
  113.1 18.1 %all-to-all-start.2 = ((f32[32,4,384]{2,1,0:T(4,128)}), f32[32,4,384]{2,1,0:T(4,128)S(1)}, u32[]{:S(2)}, u32[]{:S(2)}) async-start(f32[32,4,384]{2,1,0:T(4,128)} %shard_map.59), calls=%async_computation.2 | async-start | bytes 393216 | tf_op jit(solution)/shard_map/all_to_all | solution.py:187
  121.8 15.2 %collective-permute-start.15 = (f32[128,384]{1,0:T(8,128)S(1)}, f32[128,384]{1,0:T(8,128)S(1)}, u32[]{:S(2)}, u32[]{:S(2)}) collective-permute-start(f32[128,384]{1,0:T(8,128)S(1)} %get-tuple-element.41), channel_id=1, source_target_pairs={{0,8},{8,16},{16,24},{24,0},{32,56},{40,32},{48,40},{56,48},{1,9},... | collective-permute-start | bytes 589832 | tf_op jit(solution)/shard_map/ppermute | solution.py:193
  126.2 10.8 %collective-permute-start.16 = (f32[128,384]{1,0:T(8,128)S(1)}, f32[128,384]{1,0:T(8,128)S(1)}, u32[]{:S(2)}, u32[]{:S(2)}) collective-permute-start(f32[128,384]{1,0:T(8,128)S(1)} %get-tuple-element.42), channel_id=1, source_target_pairs={{0,16},{8,24},{16,0},{24,8},{32,48},{40,56},{48,32},{56,40},{1,17}... | collective-permute-start | bytes 589832 | tf_op jit(solution)/shard_map/ppermute | solution.py:193
  128.6 10.9 %collective-permute-start.17 = (f32[128,384]{1,0:T(8,128)S(1)}, f32[128,384]{1,0:T(8,128)S(1)}, u32[]{:S(2)}, u32[]{:S(2)}) collective-permute-start(f32[128,384]{1,0:T(8,128)S(1)} %get-tuple-element.43), channel_id=1, source_target_pairs={{0,24},{8,0},{16,8},{24,16},{32,40},{40,48},{48,56},{56,32},{1,25}... | collective-permute-start | bytes 589832 | tf_op jit(solution)/shard_map/ppermute | solution.py:193
  131.2 13.2 %collective-permute-start.18 = (f32[32,4,384]{2,1,0:T(4,128)S(1)}, f32[32,4,384]{2,1,0:T(4,128)S(1)}, u32[]{:S(2)}, u32[]{:S(2)}) collective-permute-start(f32[32,4,384]{2,1,0:T(4,128)S(1)} %all-to-all-done.2.after_ref.mine_ref), channel_id=1, source_target_pairs={{0,32},{32,0},{1,33},{33,1},{2,34},{34,2},{3,35},{35,3},{4,36},{36... | collective-permute-start | bytes 589832 | tf_op jit(solution)/shard_map/ppermute | solution.py:201
  140.5 3.8 %copy-start.3 = (f32[384,384]{1,0:T(8,128)S(1)}, f32[384,384]{1,0:T(8,128)}, u32[]{:S(2)}) copy-start(f32[384,384]{1,0:T(8,128)} %arrow_ref.1) | copy-start | bytes 1769476
  140.5 17.1 %all-to-all-start.3 = ((f32[4,128,384]{2,1,0:T(8,128)}), f32[4,128,384]{2,1,0:T(8,128)S(1)}, u32[]{:S(2)}, u32[]{:S(2)}) async-start(f32[4,128,384]{2,1,0:T(8,128)} %shard_map.60.after_ref), calls=%async_computation.3 | async-start | bytes 1572864 | tf_op jit(solution)/shard_map/all_to_all | solution.py:187

commit v5 on v3

v5 whole, which is shorter than its diff:
```python
import functools

import jax
import jax.numpy as jnp
from jax import lax
from jax.experimental import pallas as pl
from jax.experimental.pallas import tpu as pltpu
from jax.sharding import Mesh, PartitionSpec as P

B = 4096
PLANE = ("row", "col")


PANEL = 8


def dot32(a, b, left=1, right=0):
    return lax.dot_general(
        a,
        b,
        (((left,), (right,)), ((), ())),
        precision=lax.Precision.HIGHEST,
        preferred_element_type=jnp.float32,
    )


def block_inverse(m):
    n, w = m.shape[0], PANEL
    lane = lax.broadcasted_iota(jnp.int32, (n, n), 1)
    panel_lane = lax.broadcasted_iota(jnp.int32, (w, n), 1)
    sub = lax.broadcasted_iota(jnp.int32, (w, n), 0)
    for k in range(0, n, w):
        rows = m[k : k + w, :]
        cols = [jnp.broadcast_to(rows[:, k + j : k + j + 1], (w, n)) for j in range(w)]
        inside = (panel_lane >= k) & (panel_lane < k + w)
        t = jnp.where(inside, jnp.where(panel_lane == sub + k, 1.0, 0.0), rows)
        for j in range(w):
            inv = 1.0 / cols[j][j : j + 1, :]
            pivot = t[j : j + 1, :] * inv
            t = jnp.where(sub == j, pivot, t - cols[j] * pivot)
            for i in range(j + 1, w):
                p = cols[i][j : j + 1, :] * inv
                cols[i] = jnp.where(sub == j, p, cols[i] - cols[j] * p)
        new = jnp.where((lane >= k) & (lane < k + w), 0.0, m)
        for j in range(w):
            new = new - m[:, k + j : k + j + 1] * t[j : j + 1, :]
        m = jnp.concatenate([x for x in (new[:k], t, new[k + w :]) if x.shape[0]])
    return m


def gram_kernel(mine_ref, other_ref, pieces_ref):
    weights = jnp.concatenate([mine_ref[...], other_ref[...]])
    n = weights.shape[1] // 3
    count, piece = pieces_ref.shape[0] // 2, pieces_ref.shape[1]
    upper = [
        lax.dot_general(
            weights[:, i * n : (i + 1) * n],
            weights[:, i * n :],
            (((0,), (0,)), ((), ())),
            preferred_element_type=jnp.float32,
        )
        for i in range(3)
    ]
    for row, block_row in enumerate((upper[0], jnp.concatenate(upper[1:], axis=1))):
        for i in range(count):
            pieces_ref[row * count + i] = block_row[i * piece : (i + 1) * piece]


def turned(axis, distance):
    n = lax.axis_size(axis)
    steps = jnp.where(lax.axis_index("core") == 0, distance % n, -distance % n)
    return lax.rem(lax.axis_index(axis) + steps, n)


def chunk(axis, distance, size):
    return pl.ds(pl.multiple_of(turned(axis, distance) * size, size), size)


def pair_kernel(mine_ref, other_ref, copies_ref):
    fan_out(jnp.concatenate([other_ref[...], mine_ref[...]]), copies_ref)


def map_kernel(mine_ref, other_ref, gathered_ref, out_ref, weights_ref):
    n = gathered_ref.shape[1] // 2
    m = out_ref.shape[1] // 2
    for part, factor_ref in enumerate((other_ref, mine_ref)):
        for i in range(gathered_ref.shape[0]):
            weights_ref[i * n : (i + 1) * n] = gathered_ref[i, part * n : (part + 1) * n]
        for i in range(out_ref.shape[0]):
            out_ref[i, part * m : (part + 1) * m] = -lax.dot_general(
                factor_ref[:, i * m : (i + 1) * m],
                weights_ref[...],
                (((0,), (0,)), ((), ())),
                preferred_element_type=jnp.float32,
            )


def part_kernel(both_ref, mine_ref, other_ref):
    m = both_ref.shape[1] // 2
    for i in range(both_ref.shape[0]):
        other_ref[i * m : (i + 1) * m] = both_ref[i, :m]
        mine_ref[i * m : (i + 1) * m] = both_ref[i, m:]


def sum_of(ref):
    total = ref[0]
    for i in range(1, ref.shape[0]):
        total = total + ref[i]
    return total


def fan_out(x, copies_ref):
    for i in range(copies_ref.shape[0]):
        copies_ref[i] = x


def sum_kernel(parts_ref, copies_ref):
    fan_out(sum_of(parts_ref), copies_ref)


def inverse_kernel(scale, packed_ref, arrow_ref, out_ref, spare_ref):
    size = arrow_ref.shape[0]
    n = size // 3
    s = [slice(i * n, (i + 1) * n) for i in range(3)]

    def block(i, j):
        gram = packed_ref[s[0], s[j]] if i == 0 else packed_ref[s[1], s[i + j - 2]]
        return (arrow_ref[s[i], s[j]] - gram) * scale

    p0 = block_inverse(block(0, 0))
    a0 = jnp.concatenate([block(0, 1), block(0, 2)], axis=1)
    t0 = dot32(p0, a0)
    low = dot32(a0, t0, 0, 0)
    p1 = block_inverse(block(1, 1) - low[:n, :n])
    a1 = block(1, 2) - low[:n, n:]
    t1 = dot32(p1, a1)
    p2 = block_inverse(block(2, 2) - low[n:, n:] - dot32(a1, t1, 0, 0))
    x12 = -dot32(t1, p2)
    x11 = p1 - dot32(x12, t1, 1, 1)
    rest = jnp.concatenate(
        [jnp.concatenate([x11, x12], axis=1), jnp.concatenate([x12.T, p2], axis=1)]
    )
    x0 = -dot32(t0, rest)
    out_ref[s[0], s[0]] = p0 - dot32(x0, t0, 1, 1)
    out_ref[s[0], n:] = x0
    out_ref[n:size, s[0]] = x0.T
    out_ref[n:size, n:] = rest
    out_ref[size:] = jnp.zeros_like(out_ref[size:])
    spare_ref[...] = jnp.zeros_like(spare_ref)


VMEM = pl.BlockSpec(memory_space=pltpu.VMEM)
LATER = pl.BlockSpec(memory_space=pl.ANY)


def call(kernel, out_shape, in_specs, flops, scratch=()):
    return pl.pallas_call(
        kernel,
        out_shape=out_shape,
        in_specs=in_specs,
        out_specs=jax.tree.map(lambda _: VMEM, out_shape),
        scratch_shapes=scratch,
        compiler_params=pltpu.CompilerParams(vmem_limit_bytes=16 * 2**20),
        cost_estimate=pl.CostEstimate(flops=flops, bytes_accessed=2**20, transcendentals=0),
    )


def exchange(pieces, axes):
    return lax.all_to_all(pieces, axes, 0, 0, tiled=True)


def shift(x, axis, distance):
    n = lax.axis_size(axis)
    ways = ((0, distance), (n, -distance))
    return lax.ppermute(
        x,
        ("core", axis),
        [(first + i, first + (i + d) % n) for first, d in ways for i in range(n)],
    )


def swap(x):
    return lax.ppermute(x, "core", [(0, 1), (1, 0)])


def ring_rows(distance, rows):
    return turned("col", distance) * rows


def far_kernel(*refs):
    factors, couplings, (half_ref, third_ref) = refs[:2], refs[2:4], refs[4:6]
    rows_ref, nodes_ref, ready = refs[6:]
    part_rows, rows = half_ref.shape[1], third_ref.shape[1]
    half = ring_rows(4, rows) + lax.axis_index("core") * part_rows
    copies = []
    for part in range(2):
        for source, target in (
            (factors[part].at[pl.ds(pl.multiple_of(half, part_rows), part_rows), :],
             rows_ref.at[part, pl.ds(0, part_rows), :]),
            (factors[part].at[pl.ds(pl.multiple_of(ring_rows(3, rows), rows), rows), :],
             rows_ref.at[part, pl.ds(part_rows, rows), :]),
            (couplings[part], nodes_ref.at[part]),
        ):
            copies.append(pltpu.make_async_copy(source, target, ready.at[len(copies)]))
    for copy in copies:
        copy.start()
    for copy in copies:
        copy.wait()
    for part in range(2):
        products = jnp.dot(
            rows_ref[part], nodes_ref[part], preferred_element_type=jnp.float32
        )
        half_ref[part] = products[:part_rows]
        third_ref[part] = products[part_rows:]


def near_kernel(*refs):
    factors, couplings, out_refs = refs[:2], refs[2:4], refs[5:]
    for distance, out_ref in zip((1, 2, 0), out_refs):
        rows = out_ref.shape[1]
        first = pl.multiple_of(ring_rows(distance, rows), rows)
        for part in range(2):
            out_ref[part] = jnp.dot(
                factors[part][pl.ds(first, rows), :],
                couplings[part][...],
                preferred_element_type=jnp.float32,
            )


def merge_kernel(second_ref, third_ref, half_ref, out_ref):
    out_ref[...] = second_ref[...] + third_ref[...]
    size = half_ref.shape[1]
    rows = pl.ds(pl.multiple_of(lax.axis_index("core") * size, size), size)
    for part in range(half_ref.shape[0]):
        out_ref[part, rows, :] = out_ref[part, rows, :] + half_ref[part]


def add_kernel(a_ref, b_ref, out_ref):
    out_ref[...] = a_ref[...] + b_ref[...]


def last_kernel(own_ref, mine_ref, received_ref, weights_ref, other_ref):
    for part, out_ref in enumerate((weights_ref, other_ref)):
        total = own_ref[part] + (mine_ref[part] + received_ref[1 - part])
        out_ref[...] = total.astype(out_ref.dtype)


def ring_weights(factors, couplings):
    shape = jax.ShapeDtypeStruct
    rows = factors[0].shape[0] // lax.axis_size("col")
    width = couplings[0].shape[1]
    full = shape((2, rows, width), jnp.float32)
    operands = (*factors, *couplings)
    nodes, dtype = factors[0].shape[1], factors[0].dtype
    half, third = call(
        far_kernel,
        (shape((2, rows // 2, width), jnp.float32), full),
        [LATER] * 4,
        10**8,
        [
            pltpu.VMEM((2, 3 * rows // 2, nodes), dtype),
            pltpu.VMEM((2, nodes, width), dtype),
            pltpu.SemaphoreType.DMA((6,)),
        ],
    )(*operands)
    after, second, own = call(near_kernel, (full,) * 3, [VMEM] * 4 + [LATER], 10**8)(
        *operands, half
    )
    half, third = shift(half, "col", 2), shift(third, "col", 1)
    second = call(merge_kernel, full, [VMEM] * 3, 10**7)(second, third, half)
    total = call(add_kernel, full, [VMEM] * 2, 10**7)(
        shift(after, "col", 1), shift(second, "col", 2)
    )
    weights = shape((rows, width), jnp.bfloat16)
    return call(last_kernel, (weights,) * 2, [VMEM] * 3, 10**7)(own, total, swap(total))


def covariance_branch(weights, other, factor, other_factor, arrow_block):
    del other_factor
    f32 = jnp.float32
    shape = jax.ShapeDtypeStruct
    planes, size = lax.axis_size("z"), lax.axis_size(PLANE)
    width = weights.shape[1]
    piece = (2 * width // 3 // size, width)
    parts = call(gram_kernel, shape((size,) + piece, f32), [VMEM] * 2, 10**9)(weights, other)
    parts = exchange(parts, PLANE)
    parts = call(sum_kernel, shape((planes,) + piece, f32), [VMEM], 10**7)(parts)
    parts = exchange(parts, "z")
    parts = call(sum_kernel, shape((size,) + piece, f32), [VMEM], 10**7)(parts)
    packed = exchange(parts, PLANE).reshape(-1, width)
    covariance, spare = call(
        functools.partial(inverse_kernel, 1.0 / (planes * lax.axis_size("core") * B)),
        (shape((factor.shape[1], width), f32),) * 2,
        [VMEM] * 2,
        15 * 10**9,
    )(packed, arrow_block)
    return spare, covariance


def map_branch(weights, other, factor, other_factor, arrow_block):
    del arrow_block
    f32 = jnp.float32
    shape = jax.ShapeDtypeStruct
    cols, rows = lax.axis_size("col"), lax.axis_size("row")
    height, width = weights.shape
    copies = call(
        pair_kernel, shape((cols, 2 * height, width), weights.dtype), [VMEM] * 2, 10**7
    )(weights, other)
    gathered = exchange(copies, "col")
    both = shape((rows, 2 * factor.shape[1] // rows, width), f32)
    parts = call(
        map_kernel,
        both,
        [VMEM] * 3,
        2 * 10**9,
        [pltpu.VMEM((cols * height, width), weights.dtype)],
    )(factor, other_factor, gathered)
    copies = call(sum_kernel, both, [VMEM], 10**7)(exchange(parts, "row"))
    maps = exchange(copies, "row")
    return call(part_kernel, (shape((factor.shape[1], width), f32),) * 2, [VMEM], 10**7)(maps)


def per_device(factor_inverse, coupling, arrow_block):
    other_factor = swap(factor_inverse)
    weights, other = ring_weights((factor_inverse, other_factor), (coupling, swap(coupling)))
    mine, sent = lax.cond(
        lax.axis_index("core") == 0,
        covariance_branch,
        map_branch,
        weights,
        other,
        factor_inverse,
        other_factor,
        arrow_block,
    )
    received = swap(sent)
    first = lax.axis_index("core") == 0
    rows = arrow_block.shape[0]
    return (
        jnp.where(first, received, mine),
        jnp.where(first, sent[:rows], received[:rows]),
    )


def solution(mesh):
    tm, row, col = mesh.devices.shape
    split = Mesh(mesh.devices.reshape(tm // 2, 2, row, col), ("z", "core") + PLANE)
    blocks = P(("z", "core", "col"), None)
    return jax.shard_map(
        per_device,
        mesh=split,
        in_specs=(P(("z", "core", "row"), "col"), blocks, P()),
        out_specs=(blocks, P()),
        check_vma=False,
    )
```

time: 181 us -> 140 us (0.77)
  waiting for transfers between devices: 66.3 us -> 21.4 us
  starting transfers between devices: 17.7 us -> 47.4 us
  between operations: 13.8 us -> 0.75 us
  Pallas kernels: 16.1 us -> 3.88 us
  blocking collectives: 57.2 us -> 62.5 us
  local copies, waits for them, and re-layouts: 4.17 us -> 1 us
  matrix products: 3.1 us -> 0 us
    reduce_scatter x2 -> x0, waiting for transfers between devices: 65.2 us -> none  [the longest x1 53.3 us: per_device(): lax.psum_scatter(jnp.dot(factor_inverse, coupling, preferred_element_type...]
    ppermute x2 -> x4, starting transfers between devices: 13.9 us -> 38.7 us  [swap(): return lax.ppermute(x, 'core', [(0, 1), (1, 0)])]
    ppermute x0 -> x4, waiting for transfers between devices: none -> 16.3 us  [shift(): lax.ppermute(x, ('core', axis), [(first + i, first + (i + d) % n) for fir...]
    pallas_call x6 -> x9, Pallas kernels: 16.1 us -> 3.88 us  [the longest x1 1.44 us: ring_weights(): call(far_kernel, (shape((2, rows // 2, width), jnp.float32), full), [LATE...]
    ppermute x0 -> x4, starting transfers between devices: none -> 8.73 us  [shift(): lax.ppermute(x, ('core', axis), [(first + i, first + (i + d) % n) for fir...]
    all_to_all x3, blocking collectives: 57.2 us -> 62.5 us  [exchange(): return lax.all_to_all(pieces, axes, 0, 0, tiled=True)]
    ppermute x2 -> x4, waiting for transfers between devices: 0.92 us -> 5.11 us  [swap(): return lax.ppermute(x, 'core', [(0, 1), (1, 0)])]
    all_to_all x1 -> x0, starting transfers between devices: 3.67 us -> none  [exchange(): return lax.all_to_all(pieces, axes, 0, 0, tiled=True)]
  transfers between devices with their start and end apart: 6 -> 8, of which waited for: 4 -> 6; matrix products, arithmetic and copies ran while one was open for 1% -> 0% of each run, Pallas kernels for 8% -> 0%
where the time goes in v5:
time: 140 us; the launch traced here: 139 us
  blocking collectives  62.5 us (45%)
  starting transfers between devices  47.4 us (34%)
  waiting for transfers between devices  21.4 us (15%)
  Pallas kernels  3.88 us (3%)
  other arithmetic  1.84 us (1%)
    all_to_all x3, blocking collectives, exchange(): return lax.all_to_all(pieces, axes, 0, 0, tiled=True)  62.5 us
    ppermute x4, starting transfers between devices, swap(): return lax.ppermute(x, 'core', [(0, 1), (1, 0)])  38.7 us
    ppermute x4, waiting for transfers between devices, shift(): lax.ppermute(x, ('core', axis), [(first + i, first + (i + d) % n) for fir...  16.3 us
    ppermute x4, starting transfers between devices, shift(): lax.ppermute(x, ('core', axis), [(first + i, first + (i + d) % n) for fir...  8.73 us
    ppermute x4, waiting for transfers between devices, swap(): return lax.ppermute(x, 'core', [(0, 1), (1, 0)])  5.11 us
  transfers between devices with their start and end apart: 8, of which 6 were waited for; matrix products, arithmetic and copies ran while one was open for 0% of the time, Pallas kernels for 0%

profile of v5, /device:TPU:1, one launch (start us, length us, event | category | flops | bytes accessed | tf_op | source)
XLA Modules:
  0.0 139.0 jit_solution(13717009373770863539)
XLA Ops:
  0.6 16.1 %collective-permute-start = (bf16[1024,512]{1,0:T(8,128)(2,1)}, bf16[1024,512]{1,0:T(8,128)(2,1)S(1)}, u32[]{:S(2)}, u32[]{:S(2)}) collective-permute-start(bf16[1024,512]{1,0:T(8,128)(2,1)} %refs_0_.3), channel_id=1, source_target_pairs={{0,32},{32,0},{1,33},{33,1},{2,34},{34,2},{3,35},{35,3},{4,36},{36... | collective-permute-start | bytes 3145736 | tf_op jit(solution)/shard_map/ppermute | solution.py:183
  16.7 1.9 %collective-permute-start.1 = (bf16[512,384]{1,0:T(8,128)(2,1)}, bf16[512,384]{1,0:T(8,128)(2,1)S(1)}, u32[]{:S(2)}, u32[]{:S(2)}) collective-permute-start(bf16[512,384]{1,0:T(8,128)(2,1)} %refs_2_.3), channel_id=1, source_target_pairs={{0,32},{32,0},{1,33},{33,1},{2,34},{34,2},{3,35},{35,3},{4,36},{36... | collective-permute-start | bytes 1179656 | tf_op jit(solution)/shard_map/ppermute | solution.py:183
  18.6 1.9 %collective-permute-done.1.refs_3_ = bf16[512,384]{1,0:T(8,128)(2,1)S(1)} collective-permute-done((bf16[512,384]{1,0:T(8,128)(2,1)}, bf16[512,384]{1,0:T(8,128)(2,1)S(1)}, u32[]{:S(2)}, u32[]{:S(2)}) %collective-permute-start.1) | collective-permute-done | bytes 393248 | tf_op jit(solution)/shard_map/ppermute | solution.py:183
  20.5 0.0 collective-permute-done.refs_1_
  20.5 0.0 copy-start
  20.5 1.0 copy-done
  21.5 0.0 copy-start.1
  21.5 1.4 %shard_map.51 = (f32[2,64,384]{2,1,0:T(8,128)S(1)}, f32[2,128,384]{2,1,0:T(8,128)S(1)}) custom-call(bf16[1024,512]{1,0:T(8,128)(2,1)} %refs_0_.3, bf16[1024,512]{1,0:T(8,128)(2,1)S(1)} %collective-permute-done.refs_1_, bf16[512,384]{1,0:T(8,128)(2,1)S(1)} %copy-done, bf16[512,384]{1,0:T(8,128)(2,1)S(1)} %collective-permute-done.1.refs_3_), custom_call_target="tpu_custom_call" | custom-call | flops 100000000 | bytes 1048576 | tf_op jit(solution)/shard_map/pallas_call | solution.py:255
  23.0 1.9 %collective-permute-start.3 = (f32[2,128,384]{2,1,0:T(8,128)S(1)}, f32[2,128,384]{2,1,0:T(8,128)S(1)}, u32[]{:S(2)}, u32[]{:S(2)}) collective-permute-start(f32[2,128,384]{2,1,0:T(8,128)S(1)} %get-tuple-element.48), channel_id=1, source_target_pairs={{0,1},{1,2},{2,3},{3,4},{4,5},{5,6},{6,7},{7,0},{32,39},{33,32},{3... | collective-permute-start | bytes 1179656 | tf_op jit(solution)/shard_map/ppermute | solution.py:175
  24.9 1.9 %collective-permute-start.4 = (f32[2,64,384]{2,1,0:T(8,128)S(1)}, f32[2,64,384]{2,1,0:T(8,128)S(1)}, u32[]{:S(2)}, u32[]{:S(2)}) collective-permute-start(f32[2,64,384]{2,1,0:T(8,128)S(1)} %get-tuple-element.44.refs_4_), channel_id=1, source_target_pairs={{0,2},{1,3},{2,4},{3,5},{4,6},{5,7},{6,0},{7,1},{32,38},{33,39},{3... | collective-permute-start | bytes 589832 | tf_op jit(solution)/shard_map/ppermute | solution.py:175
  26.8 0.0 copy-done.1
  26.8 0.6 shard_map.52
  27.4 1.9 %collective-permute-start.2 = (f32[2,128,384]{2,1,0:T(8,128)S(1)}, f32[2,128,384]{2,1,0:T(8,128)S(1)}, u32[]{:S(2)}, u32[]{:S(2)}) collective-permute-start(f32[2,128,384]{2,1,0:T(8,128)S(1)} %get-tuple-element.46), channel_id=1, source_target_pairs={{0,1},{1,2},{2,3},{3,4},{4,5},{5,6},{6,7},{7,0},{32,39},{33,32},{3... | collective-permute-start | bytes 1179656 | tf_op jit(solution)/shard_map/ppermute | solution.py:175
  29.4 5.3 %collective-permute-done.4.half_ref = f32[2,64,384]{2,1,0:T(8,128)S(1)} collective-permute-done((f32[2,64,384]{2,1,0:T(8,128)S(1)}, f32[2,64,384]{2,1,0:T(8,128)S(1)}, u32[]{:S(2)}, u32[]{:S(2)}) %collective-permute-start.4) | collective-permute-done | bytes 196640 | tf_op jit(solution)/shard_map/ppermute | solution.py:175
  34.7 0.0 collective-permute-done.3.third_ref
  34.7 0.1 shard_map.53
  34.7 3.0 %collective-permute-start.5 = (f32[2,128,384]{2,1,0:T(8,128)S(1)}, f32[2,128,384]{2,1,0:T(8,128)S(1)}, u32[]{:S(2)}, u32[]{:S(2)}) collective-permute-start(f32[2,128,384]{2,1,0:T(8,128)S(1)} %shard_map.53), channel_id=1, source_target_pairs={{0,2},{1,3},{2,4},{3,5},{4,6},{5,7},{6,0},{7,1},{32,38},{33,39},{3... | collective-permute-start | bytes 1179656 | tf_op jit(solution)/shard_map/ppermute | solution.py:175
  37.7 2.5 %collective-permute-done.2.a_ref = f32[2,128,384]{2,1,0:T(8,128)S(1)} collective-permute-done((f32[2,128,384]{2,1,0:T(8,128)S(1)}, f32[2,128,384]{2,1,0:T(8,128)S(1)}, u32[]{:S(2)}, u32[]{:S(2)}) %collective-permute-start.2) | collective-permute-done | bytes 393248 | tf_op jit(solution)/shard_map/ppermute | solution.py:175
  40.2 8.5 %collective-permute-done.5.b_ref = f32[2,128,384]{2,1,0:T(8,128)S(1)} collective-permute-done((f32[2,128,384]{2,1,0:T(8,128)S(1)}, f32[2,128,384]{2,1,0:T(8,128)S(1)}, u32[]{:S(2)}, u32[]{:S(2)}) %collective-permute-start.5) | collective-permute-done | bytes 393248 | tf_op jit(solution)/shard_map/ppermute | solution.py:175
  48.8 6.0 %collective-permute-start.6 = (f32[2,128,384]{2,1,0:T(8,128)S(1)}, f32[2,128,384]{2,1,0:T(8,128)S(1)}, u32[]{:S(2)}, u32[]{:S(2)}) collective-permute-start(f32[2,128,384]{2,1,0:T(8,128)S(1)} %shard_map.54.mine_ref), channel_id=1, source_target_pairs={{0,32},{32,0},{1,33},{33,1},{2,34},{34,2},{3,35},{35,3},{4,36},{36... | collective-permute-start | bytes 1179656 | tf_op jit(solution)/shard_map/ppermute | solution.py:183
  54.8 1.3 collective-permute-done.6.received_ref
  56.1 0.1 shard_map.55
  56.2 64.4 %conditional.1 = ((f32[512,384]{1,0:T(8,128)S(1)}, f32[512,384]{1,0:T(8,128)S(1)})) conditional(s32[]{:T(128)} %convert_element_type.3, (bf16[128,384]{1,0:T(8,128)(2,1)S(1)}, bf16[128,384]{1,0:T(8,128)(2,1)S(1)}, bf16[1024,512]{1,0:T(8,128)(2,1)S(1)}, bf16[1024,512]{1,0:T(8,128)(2,1)S(1)}) %tuple.37, (bf16[128,384]{1,0:T(8,128)(2,1)S(1)}, ...), branch_computations={%region_0.0_spmd, %region_1.0_spmd} | conditional | flops 16020000768 | bytes 13631496 | solution.py:326
  56.2 0.1 branch_0_fun.4
  56.4 30.0 %all_to_all.24.gathered_ref = bf16[8,256,384]{2,1,0:T(8,128)(2,1)S(1)} all-to-all(bf16[8,256,384]{2,1,0:T(8,128)(2,1)S(1)} %branch_0_fun.4), channel_id=1, replica_groups=mesh['z'=16,'core'=2,'row'=4,'col'=8] {'col'}, dimensions={0} | all-to-all | bytes 3145728 | tf_op jit(solution)/shard_map/cond/branch_0_fun/all_to_all | solution.py:169
  86.4 1.4 branch_0_fun.5
  87.8 15.3 %all_to_all.25.parts_ref = f32[4,256,384]{2,1,0:T(8,128)S(1)} all-to-all(f32[4,256,384]{2,1,0:T(8,128)S(1)} %branch_0_fun.5), channel_id=1, replica_groups=mesh['z'=16,'core'=2,'row'=4,'col'=8] {'row'}, dimensions={0} | all-to-all | bytes 3145728 | tf_op jit(solution)/shard_map/cond/branch_0_fun/all_to_all | solution.py:169
  103.0 0.1 branch_0_fun.6
  103.2 17.1 %all_to_all.26.both_ref = f32[4,256,384]{2,1,0:T(8,128)S(1)} all-to-all(f32[4,256,384]{2,1,0:T(8,128)S(1)} %branch_0_fun.6), channel_id=1, replica_groups=mesh['z'=16,'core'=2,'row'=4,'col'=8] {'row'}, dimensions={0} | all-to-all | bytes 3145728 | tf_op jit(solution)/shard_map/cond/branch_0_fun/all_to_all | solution.py:169
  120.3 0.1 branch_0_fun.7
  120.6 14.6 %collective-permute-start.7 = (f32[512,384]{1,0:T(8,128)S(1)}, f32[512,384]{1,0:T(8,128)S(1)}, u32[]{:S(2)}, u32[]{:S(2)}) collective-permute-start(f32[512,384]{1,0:T(8,128)S(1)} %get-tuple-element.59), channel_id=1, source_target_pairs={{0,32},{32,0},{1,33},{33,1},{2,34},{34,2},{3,35},{35,3},{4,36},{36... | collective-permute-start | bytes 2359304 | tf_op jit(solution)/shard_map/ppermute | solution.py:183
  135.3 1.9 %collective-permute-done.7 = f32[512,384]{1,0:T(8,128)S(1)} collective-permute-done((f32[512,384]{1,0:T(8,128)S(1)}, f32[512,384]{1,0:T(8,128)S(1)}, u32[]{:S(2)}, u32[]{:S(2)}) %collective-permute-start.7) | collective-permute-done | bytes 786464 | tf_op jit(solution)/shard_map/ppermute | solution.py:183
  137.2 0.9 slice_select_fusion
  138.0 1.0 broadcast_select_fusion
  (1 shorter events, 0.0 us)
Async XLA Ops:
  0.6 19.9 %collective-permute-start = (bf16[1024,512]{1,0:T(8,128)(2,1)}, bf16[1024,512]{1,0:T(8,128)(2,1)S(1)}, u32[]{:S(2)}, u32[]{:S(2)}) collective-permute-start(bf16[1024,512]{1,0:T(8,128)(2,1)} %refs_0_.3), channel_id=1, source_target_pairs={{0,32},{32,0},{1,33},{33,1},{2,34},{34,2},{3,35},{35,3},{4,36},{36... | collective-permute-start | bytes 3145736 | tf_op jit(solution)/shard_map/ppermute | solution.py:183
  16.7 3.8 %collective-permute-start.1 = (bf16[512,384]{1,0:T(8,128)(2,1)}, bf16[512,384]{1,0:T(8,128)(2,1)S(1)}, u32[]{:S(2)}, u32[]{:S(2)}) collective-permute-start(bf16[512,384]{1,0:T(8,128)(2,1)} %refs_2_.3), channel_id=1, source_target_pairs={{0,32},{32,0},{1,33},{33,1},{2,34},{34,2},{3,35},{35,3},{4,36},{36... | collective-permute-start | bytes 1179656 | tf_op jit(solution)/shard_map/ppermute | solution.py:183
  20.5 1.0 copy-start
  21.5 5.3 %copy-start.1 = (bf16[1024,512]{1,0:T(8,128)(2,1)S(1)}, bf16[1024,512]{1,0:T(8,128)(2,1)}, u32[]{:S(2)}) copy-start(bf16[1024,512]{1,0:T(8,128)(2,1)} %refs_0_.3) | copy-start | bytes 3145732
  23.0 11.7 %collective-permute-start.3 = (f32[2,128,384]{2,1,0:T(8,128)S(1)}, f32[2,128,384]{2,1,0:T(8,128)S(1)}, u32[]{:S(2)}, u32[]{:S(2)}) collective-permute-start(f32[2,128,384]{2,1,0:T(8,128)S(1)} %get-tuple-element.48), channel_id=1, source_target_pairs={{0,1},{1,2},{2,3},{3,4},{4,5},{5,6},{6,7},{7,0},{32,39},{33,32},{3... | collective-permute-start | bytes 1179656 | tf_op jit(solution)/shard_map/ppermute | solution.py:175
  24.9 9.8 %collective-permute-start.4 = (f32[2,64,384]{2,1,0:T(8,128)S(1)}, f32[2,64,384]{2,1,0:T(8,128)S(1)}, u32[]{:S(2)}, u32[]{:S(2)}) collective-permute-start(f32[2,64,384]{2,1,0:T(8,128)S(1)} %get-tuple-element.44.refs_4_), channel_id=1, source_target_pairs={{0,2},{1,3},{2,4},{3,5},{4,6},{5,7},{6,0},{7,1},{32,38},{33,39},{3... | collective-permute-start | bytes 589832 | tf_op jit(solution)/shard_map/ppermute | solution.py:175
  27.4 12.8 %collective-permute-start.2 = (f32[2,128,384]{2,1,0:T(8,128)S(1)}, f32[2,128,384]{2,1,0:T(8,128)S(1)}, u32[]{:S(2)}, u32[]{:S(2)}) collective-permute-start(f32[2,128,384]{2,1,0:T(8,128)S(1)} %get-tuple-element.46), channel_id=1, source_target_pairs={{0,1},{1,2},{2,3},{3,4},{4,5},{5,6},{6,7},{7,0},{32,39},{33,32},{3... | collective-permute-start | bytes 1179656 | tf_op jit(solution)/shard_map/ppermute | solution.py:175
  34.7 14.0 %collective-permute-start.5 = (f32[2,128,384]{2,1,0:T(8,128)S(1)}, f32[2,128,384]{2,1,0:T(8,128)S(1)}, u32[]{:S(2)}, u32[]{:S(2)}) collective-permute-start(f32[2,128,384]{2,1,0:T(8,128)S(1)} %shard_map.53), channel_id=1, source_target_pairs={{0,2},{1,3},{2,4},{3,5},{4,6},{5,7},{6,0},{7,1},{32,38},{33,39},{3... | collective-permute-start | bytes 1179656 | tf_op jit(solution)/shard_map/ppermute | solution.py:175
  48.8 7.4 %collective-permute-start.6 = (f32[2,128,384]{2,1,0:T(8,128)S(1)}, f32[2,128,384]{2,1,0:T(8,128)S(1)}, u32[]{:S(2)}, u32[]{:S(2)}) collective-permute-start(f32[2,128,384]{2,1,0:T(8,128)S(1)} %shard_map.54.mine_ref), channel_id=1, source_target_pairs={{0,32},{32,0},{1,33},{33,1},{2,34},{34,2},{3,35},{35,3},{4,36},{36... | collective-permute-start | bytes 1179656 | tf_op jit(solution)/shard_map/ppermute | solution.py:183
  120.6 16.5 %collective-permute-start.7 = (f32[512,384]{1,0:T(8,128)S(1)}, f32[512,384]{1,0:T(8,128)S(1)}, u32[]{:S(2)}, u32[]{:S(2)}) collective-permute-start(f32[512,384]{1,0:T(8,128)S(1)} %get-tuple-element.59), channel_id=1, source_target_pairs={{0,32},{32,0},{1,33},{33,1},{2,34},{34,2},{3,35},{35,3},{4,36},{36... | collective-permute-start | bytes 2359304 | tf_op jit(solution)/shard_map/ppermute | solution.py:183

commit v6 on v5

--- a/solution.py
+++ b/solution.py
@@ -76,16 +76,21 @@
     return pl.ds(pl.multiple_of(turned(axis, distance) * size, size), size)
 
 
-def pair_kernel(mine_ref, other_ref, copies_ref):
-    fan_out(jnp.concatenate([other_ref[...], mine_ref[...]]), copies_ref)
-
-
-def map_kernel(mine_ref, other_ref, gathered_ref, out_ref, weights_ref):
-    n = gathered_ref.shape[1] // 2
+def pair_kernel(first, mine_ref, other_ref, after_ref, copies_ref):
+    del after_ref
+    rows = slice(first, first + copies_ref.shape[1] // 2)
+    fan_out(jnp.concatenate([other_ref[rows], mine_ref[rows]]), copies_ref)
+
+
+def map_kernel(mine_ref, other_ref, few_ref, many_ref, out_ref, weights_ref):
     m = out_ref.shape[1] // 2
     for part, factor_ref in enumerate((other_ref, mine_ref)):
-        for i in range(gathered_ref.shape[0]):
-            weights_ref[i * n : (i + 1) * n] = gathered_ref[i, part * n : (part + 1) * n]
+        first = 0
+        for i in range(few_ref.shape[0]):
+            for ref in (few_ref, many_ref):
+                n = ref.shape[1] // 2
+                weights_ref[first : first + n] = ref[i, part * n : (part + 1) * n]
+                first += n
         for i in range(out_ref.shape[0]):
             out_ref[i, part * m : (part + 1) * m] = -lax.dot_general(
                 factor_ref[:, i * m : (i + 1) * m],
@@ -303,18 +308,26 @@
     shape = jax.ShapeDtypeStruct
     cols, rows = lax.axis_size("col"), lax.axis_size("row")
     height, width = weights.shape
-    copies = call(
-        pair_kernel, shape((cols, 2 * height, width), weights.dtype), [VMEM] * 2, 10**7
-    )(weights, other)
-    gathered = exchange(copies, "col")
+
+    def gather(first, count, after):
+        copies = call(
+            functools.partial(pair_kernel, first),
+            shape((cols, 2 * count, width), weights.dtype),
+            [VMEM, VMEM, LATER],
+            10**7,
+        )(weights, other, after)
+        return exchange(copies, "col")
+
+    few = gather(0, height // 4, weights)
+    many = gather(height // 4, height - height // 4, few)
     both = shape((rows, 2 * factor.shape[1] // rows, width), f32)
     parts = call(
         map_kernel,
         both,
-        [VMEM] * 3,
+        [VMEM] * 4,
         2 * 10**9,
         [pltpu.VMEM((cols * height, width), weights.dtype)],
-    )(factor, other_factor, gathered)
+    )(factor, other_factor, few, many)
     copies = call(sum_kernel, both, [VMEM], 10**7)(exchange(parts, "row"))
     maps = exchange(copies, "row")
     return call(part_kernel, (shape((factor.shape[1], width), f32),) * 2, [VMEM], 10**7)(maps)

time: 140 us -> 135 us (0.964)
  starting transfers between devices: 47.4 us -> 37.2 us
  blocking collectives: 62.5 us -> 68.1 us
    ppermute x4, starting transfers between devices: 38.7 us -> 28.5 us  [swap(): return lax.ppermute(x, 'core', [(0, 1), (1, 0)])]
    all_to_all x3 -> x4, blocking collectives: 62.5 us -> 68.1 us  [exchange(): return lax.all_to_all(pieces, axes, 0, 0, tiled=True)]
where the time goes in v6:
time: 135 us; the launch traced here: 134 us
  blocking collectives  68.1 us (50%)
  starting transfers between devices  37.2 us (28%)
  waiting for transfers between devices  21.4 us (16%)
  Pallas kernels  3.87 us (3%)
  other arithmetic  1.84 us (1%)
    all_to_all x4, blocking collectives, exchange(): return lax.all_to_all(pieces, axes, 0, 0, tiled=True)  68.1 us
    ppermute x4, starting transfers between devices, swap(): return lax.ppermute(x, 'core', [(0, 1), (1, 0)])  28.5 us
    ppermute x4, waiting for transfers between devices, shift(): lax.ppermute(x, ('core', axis), [(first + i, first + (i + d) % n) for fir...  16.3 us
    ppermute x4, starting transfers between devices, shift(): lax.ppermute(x, ('core', axis), [(first + i, first + (i + d) % n) for fir...  8.73 us
    ppermute x4, waiting for transfers between devices, swap(): return lax.ppermute(x, 'core', [(0, 1), (1, 0)])  5.11 us
  transfers between devices with their start and end apart: 8, of which 6 were waited for; matrix products, arithmetic and copies ran while one was open for 0% of the time, Pallas kernels for 0%

profile of v6, /device:TPU:1, one launch (start us, length us, event | category | flops | bytes accessed | tf_op | source)
XLA Modules:
  0.0 134.5 jit_solution(8731051045885192209)
XLA Ops:
  0.6 16.1 %collective-permute-start = (bf16[1024,512]{1,0:T(8,128)(2,1)}, bf16[1024,512]{1,0:T(8,128)(2,1)S(1)}, u32[]{:S(2)}, u32[]{:S(2)}) collective-permute-start(bf16[1024,512]{1,0:T(8,128)(2,1)} %refs_0_.3), channel_id=1, source_target_pairs={{0,32},{32,0},{1,33},{33,1},{2,34},{34,2},{3,35},{35,3},{4,36},{36... | collective-permute-start | bytes 3145736 | tf_op jit(solution)/shard_map/ppermute | solution.py:188
  16.7 1.9 %collective-permute-start.1 = (bf16[512,384]{1,0:T(8,128)(2,1)}, bf16[512,384]{1,0:T(8,128)(2,1)S(1)}, u32[]{:S(2)}, u32[]{:S(2)}) collective-permute-start(bf16[512,384]{1,0:T(8,128)(2,1)} %refs_2_.3), channel_id=1, source_target_pairs={{0,32},{32,0},{1,33},{33,1},{2,34},{34,2},{3,35},{35,3},{4,36},{36... | collective-permute-start | bytes 1179656 | tf_op jit(solution)/shard_map/ppermute | solution.py:188
  18.6 1.9 %collective-permute-done.1.refs_3_ = bf16[512,384]{1,0:T(8,128)(2,1)S(1)} collective-permute-done((bf16[512,384]{1,0:T(8,128)(2,1)}, bf16[512,384]{1,0:T(8,128)(2,1)S(1)}, u32[]{:S(2)}, u32[]{:S(2)}) %collective-permute-start.1) | collective-permute-done | bytes 393248 | tf_op jit(solution)/shard_map/ppermute | solution.py:188
  20.5 0.0 collective-permute-done.refs_1_
  20.5 0.0 copy-start
  20.5 1.0 copy-done
  21.5 0.0 copy-start.1
  21.5 1.4 %shard_map.51 = (f32[2,64,384]{2,1,0:T(8,128)S(1)}, f32[2,128,384]{2,1,0:T(8,128)S(1)}) custom-call(bf16[1024,512]{1,0:T(8,128)(2,1)} %refs_0_.3, bf16[1024,512]{1,0:T(8,128)(2,1)S(1)} %collective-permute-done.refs_1_, bf16[512,384]{1,0:T(8,128)(2,1)S(1)} %copy-done, bf16[512,384]{1,0:T(8,128)(2,1)S(1)} %collective-permute-done.1.refs_3_), custom_call_target="tpu_custom_call" | custom-call | flops 100000000 | bytes 1048576 | tf_op jit(solution)/shard_map/pallas_call | solution.py:260
  23.0 1.9 %collective-permute-start.3 = (f32[2,128,384]{2,1,0:T(8,128)S(1)}, f32[2,128,384]{2,1,0:T(8,128)S(1)}, u32[]{:S(2)}, u32[]{:S(2)}) collective-permute-start(f32[2,128,384]{2,1,0:T(8,128)S(1)} %get-tuple-element.48), channel_id=1, source_target_pairs={{0,1},{1,2},{2,3},{3,4},{4,5},{5,6},{6,7},{7,0},{32,39},{33,32},{3... | collective-permute-start | bytes 1179656 | tf_op jit(solution)/shard_map/ppermute | solution.py:180
  24.9 1.9 %collective-permute-start.4 = (f32[2,64,384]{2,1,0:T(8,128)S(1)}, f32[2,64,384]{2,1,0:T(8,128)S(1)}, u32[]{:S(2)}, u32[]{:S(2)}) collective-permute-start(f32[2,64,384]{2,1,0:T(8,128)S(1)} %get-tuple-element.44.refs_4_), channel_id=1, source_target_pairs={{0,2},{1,3},{2,4},{3,5},{4,6},{5,7},{6,0},{7,1},{32,38},{33,39},{3... | collective-permute-start | bytes 589832 | tf_op jit(solution)/shard_map/ppermute | solution.py:180
  26.8 0.0 copy-done.1
  26.8 0.6 shard_map.52
  27.4 1.9 %collective-permute-start.2 = (f32[2,128,384]{2,1,0:T(8,128)S(1)}, f32[2,128,384]{2,1,0:T(8,128)S(1)}, u32[]{:S(2)}, u32[]{:S(2)}) collective-permute-start(f32[2,128,384]{2,1,0:T(8,128)S(1)} %get-tuple-element.46), channel_id=1, source_target_pairs={{0,1},{1,2},{2,3},{3,4},{4,5},{5,6},{6,7},{7,0},{32,39},{33,32},{3... | collective-permute-start | bytes 1179656 | tf_op jit(solution)/shard_map/ppermute | solution.py:180
  29.4 5.3 %collective-permute-done.4.half_ref = f32[2,64,384]{2,1,0:T(8,128)S(1)} collective-permute-done((f32[2,64,384]{2,1,0:T(8,128)S(1)}, f32[2,64,384]{2,1,0:T(8,128)S(1)}, u32[]{:S(2)}, u32[]{:S(2)}) %collective-permute-start.4) | collective-permute-done | bytes 196640 | tf_op jit(solution)/shard_map/ppermute | solution.py:180
  34.7 0.0 collective-permute-done.3.third_ref
  34.7 0.1 shard_map.53
  34.7 3.0 %collective-permute-start.5 = (f32[2,128,384]{2,1,0:T(8,128)S(1)}, f32[2,128,384]{2,1,0:T(8,128)S(1)}, u32[]{:S(2)}, u32[]{:S(2)}) collective-permute-start(f32[2,128,384]{2,1,0:T(8,128)S(1)} %shard_map.53), channel_id=1, source_target_pairs={{0,2},{1,3},{2,4},{3,5},{4,6},{5,7},{6,0},{7,1},{32,38},{33,39},{3... | collective-permute-start | bytes 1179656 | tf_op jit(solution)/shard_map/ppermute | solution.py:180
  37.7 2.5 %collective-permute-done.2.a_ref = f32[2,128,384]{2,1,0:T(8,128)S(1)} collective-permute-done((f32[2,128,384]{2,1,0:T(8,128)S(1)}, f32[2,128,384]{2,1,0:T(8,128)S(1)}, u32[]{:S(2)}, u32[]{:S(2)}) %collective-permute-start.2) | collective-permute-done | bytes 393248 | tf_op jit(solution)/shard_map/ppermute | solution.py:180
  40.2 8.5 %collective-permute-done.5.b_ref = f32[2,128,384]{2,1,0:T(8,128)S(1)} collective-permute-done((f32[2,128,384]{2,1,0:T(8,128)S(1)}, f32[2,128,384]{2,1,0:T(8,128)S(1)}, u32[]{:S(2)}, u32[]{:S(2)}) %collective-permute-start.5) | collective-permute-done | bytes 393248 | tf_op jit(solution)/shard_map/ppermute | solution.py:180
  48.8 6.0 %collective-permute-start.6 = (f32[2,128,384]{2,1,0:T(8,128)S(1)}, f32[2,128,384]{2,1,0:T(8,128)S(1)}, u32[]{:S(2)}, u32[]{:S(2)}) collective-permute-start(f32[2,128,384]{2,1,0:T(8,128)S(1)} %shard_map.54.mine_ref), channel_id=1, source_target_pairs={{0,32},{32,0},{1,33},{33,1},{2,34},{34,2},{3,35},{35,3},{4,36},{36... | collective-permute-start | bytes 1179656 | tf_op jit(solution)/shard_map/ppermute | solution.py:188
  54.8 1.3 collective-permute-done.6.received_ref
  56.1 0.1 shard_map.55
  56.2 70.0 %conditional.1 = ((f32[512,384]{1,0:T(8,128)S(1)}, f32[512,384]{1,0:T(8,128)S(1)})) conditional(s32[]{:T(128)} %convert_element_type.3, (bf16[128,384]{1,0:T(8,128)(2,1)S(1)}, bf16[128,384]{1,0:T(8,128)(2,1)S(1)}, bf16[1024,512]{1,0:T(8,128)(2,1)S(1)}, bf16[1024,512]{1,0:T(8,128)(2,1)S(1)}) %tuple.37, (bf16[128,384]{1,0:T(8,128)(2,1)S(1)}, ...), branch_computations={%region_0.0_spmd, %region_1.0_spmd} | conditional | flops 16020000768 | bytes 14680072 | solution.py:339
  56.2 15.4 %all_to_all.28.after_ref.few_ref = bf16[8,64,384]{2,1,0:T(8,128)(2,1)S(1)} all-to-all(bf16[8,64,384]{2,1,0:T(8,128)(2,1)S(1)} %branch_0_fun.5), channel_id=1, replica_groups=mesh['z'=16,'core'=2,'row'=4,'col'=8] {'col'}, dimensions={0} | all-to-all | bytes 786432 | tf_op jit(solution)/shard_map/cond/branch_0_fun/all_to_all | solution.py:174
  71.7 0.1 branch_0_fun.6
  71.8 22.1 %all_to_all.29.many_ref = bf16[8,192,384]{2,1,0:T(8,128)(2,1)S(1)} all-to-all(bf16[8,192,384]{2,1,0:T(8,128)(2,1)S(1)} %branch_0_fun.6), channel_id=1, replica_groups=mesh['z'=16,'core'=2,'row'=4,'col'=8] {'col'}, dimensions={0} | all-to-all | bytes 2359296 | tf_op jit(solution)/shard_map/cond/branch_0_fun/all_to_all | solution.py:174
  93.9 1.3 %branch_0_fun.7 = f32[4,256,384]{2,1,0:T(8,128)S(1)} custom-call(bf16[1024,512]{1,0:T(8,128)(2,1)S(1)} %get-tuple-element.24.mine_ref, bf16[1024,512]{1,0:T(8,128)(2,1)S(1)} %get-tuple-element.25.other_ref, bf16[8,64,384]{2,1,0:T(8,128)(2,1)S(1)} %all_to_all.28.after_ref.few_ref, bf16[8,192,384]{2,1,0:T(8,128)(2,1)S(1)} %all_to_all.29.many_ref), custom_call_target="tpu_custom_call" | custom-call | flops 2000000000 | bytes 1048576 | tf_op jit(solution)/shard_map/cond/branch_0_fun/pallas_call | solution.py:324
  95.3 15.6 %all_to_all.30.parts_ref = f32[4,256,384]{2,1,0:T(8,128)S(1)} all-to-all(f32[4,256,384]{2,1,0:T(8,128)S(1)} %branch_0_fun.7), channel_id=1, replica_groups=mesh['z'=16,'core'=2,'row'=4,'col'=8] {'row'}, dimensions={0} | all-to-all | bytes 3145728 | tf_op jit(solution)/shard_map/cond/branch_0_fun/all_to_all | solution.py:174
  110.8 0.1 branch_0_fun.8
  110.9 15.0 %all_to_all.31.both_ref = f32[4,256,384]{2,1,0:T(8,128)S(1)} all-to-all(f32[4,256,384]{2,1,0:T(8,128)S(1)} %branch_0_fun.8), channel_id=1, replica_groups=mesh['z'=16,'core'=2,'row'=4,'col'=8] {'row'}, dimensions={0} | all-to-all | bytes 3145728 | tf_op jit(solution)/shard_map/cond/branch_0_fun/all_to_all | solution.py:174
  125.9 0.1 branch_0_fun.9
  126.2 4.5 %collective-permute-start.7 = (f32[512,384]{1,0:T(8,128)S(1)}, f32[512,384]{1,0:T(8,128)S(1)}, u32[]{:S(2)}, u32[]{:S(2)}) collective-permute-start(f32[512,384]{1,0:T(8,128)S(1)} %get-tuple-element.59), channel_id=1, source_target_pairs={{0,32},{32,0},{1,33},{33,1},{2,34},{34,2},{3,35},{35,3},{4,36},{36... | collective-permute-start | bytes 2359304 | tf_op jit(solution)/shard_map/ppermute | solution.py:188
  130.7 1.9 %collective-permute-done.7 = f32[512,384]{1,0:T(8,128)S(1)} collective-permute-done((f32[512,384]{1,0:T(8,128)S(1)}, f32[512,384]{1,0:T(8,128)S(1)}, u32[]{:S(2)}, u32[]{:S(2)}) %collective-permute-start.7) | collective-permute-done | bytes 786464 | tf_op jit(solution)/shard_map/ppermute | solution.py:188
  132.6 0.9 slice_select_fusion
  133.5 1.0 broadcast_select_fusion
  (2 shorter events, 0.1 us)
Async XLA Ops:
  0.6 19.9 %collective-permute-start = (bf16[1024,512]{1,0:T(8,128)(2,1)}, bf16[1024,512]{1,0:T(8,128)(2,1)S(1)}, u32[]{:S(2)}, u32[]{:S(2)}) collective-permute-start(bf16[1024,512]{1,0:T(8,128)(2,1)} %refs_0_.3), channel_id=1, source_target_pairs={{0,32},{32,0},{1,33},{33,1},{2,34},{34,2},{3,35},{35,3},{4,36},{36... | collective-permute-start | bytes 3145736 | tf_op jit(solution)/shard_map/ppermute | solution.py:188
  16.7 3.8 %collective-permute-start.1 = (bf16[512,384]{1,0:T(8,128)(2,1)}, bf16[512,384]{1,0:T(8,128)(2,1)S(1)}, u32[]{:S(2)}, u32[]{:S(2)}) collective-permute-start(bf16[512,384]{1,0:T(8,128)(2,1)} %refs_2_.3), channel_id=1, source_target_pairs={{0,32},{32,0},{1,33},{33,1},{2,34},{34,2},{3,35},{35,3},{4,36},{36... | collective-permute-start | bytes 1179656 | tf_op jit(solution)/shard_map/ppermute | solution.py:188
  20.5 1.0 copy-start
  21.5 5.3 %copy-start.1 = (bf16[1024,512]{1,0:T(8,128)(2,1)S(1)}, bf16[1024,512]{1,0:T(8,128)(2,1)}, u32[]{:S(2)}) copy-start(bf16[1024,512]{1,0:T(8,128)(2,1)} %refs_0_.3) | copy-start | bytes 3145732
  23.0 11.7 %collective-permute-start.3 = (f32[2,128,384]{2,1,0:T(8,128)S(1)}, f32[2,128,384]{2,1,0:T(8,128)S(1)}, u32[]{:S(2)}, u32[]{:S(2)}) collective-permute-start(f32[2,128,384]{2,1,0:T(8,128)S(1)} %get-tuple-element.48), channel_id=1, source_target_pairs={{0,1},{1,2},{2,3},{3,4},{4,5},{5,6},{6,7},{7,0},{32,39},{33,32},{3... | collective-permute-start | bytes 1179656 | tf_op jit(solution)/shard_map/ppermute | solution.py:180
  24.9 9.8 %collective-permute-start.4 = (f32[2,64,384]{2,1,0:T(8,128)S(1)}, f32[2,64,384]{2,1,0:T(8,128)S(1)}, u32[]{:S(2)}, u32[]{:S(2)}) collective-permute-start(f32[2,64,384]{2,1,0:T(8,128)S(1)} %get-tuple-element.44.refs_4_), channel_id=1, source_target_pairs={{0,2},{1,3},{2,4},{3,5},{4,6},{5,7},{6,0},{7,1},{32,38},{33,39},{3... | collective-permute-start | bytes 589832 | tf_op jit(solution)/shard_map/ppermute | solution.py:180
  27.4 12.8 %collective-permute-start.2 = (f32[2,128,384]{2,1,0:T(8,128)S(1)}, f32[2,128,384]{2,1,0:T(8,128)S(1)}, u32[]{:S(2)}, u32[]{:S(2)}) collective-permute-start(f32[2,128,384]{2,1,0:T(8,128)S(1)} %get-tuple-element.46), channel_id=1, source_target_pairs={{0,1},{1,2},{2,3},{3,4},{4,5},{5,6},{6,7},{7,0},{32,39},{33,32},{3... | collective-permute-start | bytes 1179656 | tf_op jit(solution)/shard_map/ppermute | solution.py:180
  34.7 14.0 %collective-permute-start.5 = (f32[2,128,384]{2,1,0:T(8,128)S(1)}, f32[2,128,384]{2,1,0:T(8,128)S(1)}, u32[]{:S(2)}, u32[]{:S(2)}) collective-permute-start(f32[2,128,384]{2,1,0:T(8,128)S(1)} %shard_map.53), channel_id=1, source_target_pairs={{0,2},{1,3},{2,4},{3,5},{4,6},{5,7},{6,0},{7,1},{32,38},{33,39},{3... | collective-permute-start | bytes 1179656 | tf_op jit(solution)/shard_map/ppermute | solution.py:180
  48.8 7.4 %collective-permute-start.6 = (f32[2,128,384]{2,1,0:T(8,128)S(1)}, f32[2,128,384]{2,1,0:T(8,128)S(1)}, u32[]{:S(2)}, u32[]{:S(2)}) collective-permute-start(f32[2,128,384]{2,1,0:T(8,128)S(1)} %shard_map.54.mine_ref), channel_id=1, source_target_pairs={{0,32},{32,0},{1,33},{33,1},{2,34},{34,2},{3,35},{35,3},{4,36},{36... | collective-permute-start | bytes 1179656 | tf_op jit(solution)/shard_map/ppermute | solution.py:188
  126.2 6.4 %collective-permute-start.7 = (f32[512,384]{1,0:T(8,128)S(1)}, f32[512,384]{1,0:T(8,128)S(1)}, u32[]{:S(2)}, u32[]{:S(2)}) collective-permute-start(f32[512,384]{1,0:T(8,128)S(1)} %get-tuple-element.59), channel_id=1, source_target_pairs={{0,32},{32,0},{1,33},{33,1},{2,34},{34,2},{3,35},{35,3},{4,36},{36... | collective-permute-start | bytes 2359304 | tf_op jit(solution)/shard_map/ppermute | solution.py:188

commit v7 on v6

--- a/solution.py
+++ b/solution.py
@@ -318,8 +318,8 @@
         )(weights, other, after)
         return exchange(copies, "col")
 
-    few = gather(0, height // 4, weights)
-    many = gather(height // 4, height - height // 4, few)
+    few = gather(0, height // 8, weights)
+    many = gather(height // 8, height - height // 8, few)
     both = shape((rows, 2 * factor.shape[1] // rows, width), f32)
     parts = call(
         map_kernel,

time: 135 us -> 135 us (level)
  blocking collectives: 68.1 us -> 65.8 us
  starting transfers between devices: 37.2 us -> 39.2 us
    all_to_all x4, blocking collectives: 68.1 us -> 65.8 us  [exchange(): return lax.all_to_all(pieces, axes, 0, 0, tiled=True)]
    ppermute x4, starting transfers between devices: 28.5 us -> 30.5 us  [swap(): return lax.ppermute(x, 'core', [(0, 1), (1, 0)])]
where the time goes in v7:
time: 135 us; the launch traced here: 134 us
  blocking collectives  65.8 us (49%)
  starting transfers between devices  39.2 us (29%)
  waiting for transfers between devices  21.4 us (16%)
  Pallas kernels  3.87 us (3%)
  other arithmetic  1.84 us (1%)
    all_to_all x4, blocking collectives, exchange(): return lax.all_to_all(pieces, axes, 0, 0, tiled=True)  65.8 us
    ppermute x4, starting transfers between devices, swap(): return lax.ppermute(x, 'core', [(0, 1), (1, 0)])  30.5 us
    ppermute x4, waiting for transfers between devices, shift(): lax.ppermute(x, ('core', axis), [(first + i, first + (i + d) % n) for fir...  16.3 us
    ppermute x4, starting transfers between devices, shift(): lax.ppermute(x, ('core', axis), [(first + i, first + (i + d) % n) for fir...  8.73 us
    ppermute x4, waiting for transfers between devices, swap(): return lax.ppermute(x, 'core', [(0, 1), (1, 0)])  5.11 us
  transfers between devices with their start and end apart: 8, of which 6 were waited for; matrix products, arithmetic and copies ran while one was open for 0% of the time, Pallas kernels for 0%

profile of v7, /device:TPU:1, one launch (start us, length us, event | category | flops | bytes accessed | tf_op | source)
XLA Modules:
  0.0 134.2 jit_solution(12339253204304460785)
XLA Ops:
  0.6 16.1 %collective-permute-start = (bf16[1024,512]{1,0:T(8,128)(2,1)}, bf16[1024,512]{1,0:T(8,128)(2,1)S(1)}, u32[]{:S(2)}, u32[]{:S(2)}) collective-permute-start(bf16[1024,512]{1,0:T(8,128)(2,1)} %refs_0_.3), channel_id=1, source_target_pairs={{0,32},{32,0},{1,33},{33,1},{2,34},{34,2},{3,35},{35,3},{4,36},{36... | collective-permute-start | bytes 3145736 | tf_op jit(solution)/shard_map/ppermute | solution.py:188
  16.7 1.9 %collective-permute-start.1 = (bf16[512,384]{1,0:T(8,128)(2,1)}, bf16[512,384]{1,0:T(8,128)(2,1)S(1)}, u32[]{:S(2)}, u32[]{:S(2)}) collective-permute-start(bf16[512,384]{1,0:T(8,128)(2,1)} %refs_2_.3), channel_id=1, source_target_pairs={{0,32},{32,0},{1,33},{33,1},{2,34},{34,2},{3,35},{35,3},{4,36},{36... | collective-permute-start | bytes 1179656 | tf_op jit(solution)/shard_map/ppermute | solution.py:188
  18.6 1.9 %collective-permute-done.1.refs_3_ = bf16[512,384]{1,0:T(8,128)(2,1)S(1)} collective-permute-done((bf16[512,384]{1,0:T(8,128)(2,1)}, bf16[512,384]{1,0:T(8,128)(2,1)S(1)}, u32[]{:S(2)}, u32[]{:S(2)}) %collective-permute-start.1) | collective-permute-done | bytes 393248 | tf_op jit(solution)/shard_map/ppermute | solution.py:188
  20.5 0.0 collective-permute-done.refs_1_
  20.5 0.0 copy-start
  20.5 1.0 copy-done
  21.5 0.0 copy-start.1
  21.5 1.4 %shard_map.51 = (f32[2,64,384]{2,1,0:T(8,128)S(1)}, f32[2,128,384]{2,1,0:T(8,128)S(1)}) custom-call(bf16[1024,512]{1,0:T(8,128)(2,1)} %refs_0_.3, bf16[1024,512]{1,0:T(8,128)(2,1)S(1)} %collective-permute-done.refs_1_, bf16[512,384]{1,0:T(8,128)(2,1)S(1)} %copy-done, bf16[512,384]{1,0:T(8,128)(2,1)S(1)} %collective-permute-done.1.refs_3_), custom_call_target="tpu_custom_call" | custom-call | flops 100000000 | bytes 1048576 | tf_op jit(solution)/shard_map/pallas_call | solution.py:260
  23.0 1.9 %collective-permute-start.3 = (f32[2,128,384]{2,1,0:T(8,128)S(1)}, f32[2,128,384]{2,1,0:T(8,128)S(1)}, u32[]{:S(2)}, u32[]{:S(2)}) collective-permute-start(f32[2,128,384]{2,1,0:T(8,128)S(1)} %get-tuple-element.48), channel_id=1, source_target_pairs={{0,1},{1,2},{2,3},{3,4},{4,5},{5,6},{6,7},{7,0},{32,39},{33,32},{3... | collective-permute-start | bytes 1179656 | tf_op jit(solution)/shard_map/ppermute | solution.py:180
  24.9 1.9 %collective-permute-start.4 = (f32[2,64,384]{2,1,0:T(8,128)S(1)}, f32[2,64,384]{2,1,0:T(8,128)S(1)}, u32[]{:S(2)}, u32[]{:S(2)}) collective-permute-start(f32[2,64,384]{2,1,0:T(8,128)S(1)} %get-tuple-element.44.refs_4_), channel_id=1, source_target_pairs={{0,2},{1,3},{2,4},{3,5},{4,6},{5,7},{6,0},{7,1},{32,38},{33,39},{3... | collective-permute-start | bytes 589832 | tf_op jit(solution)/shard_map/ppermute | solution.py:180
  26.8 0.0 copy-done.1
  26.8 0.6 shard_map.52
  27.4 1.9 %collective-permute-start.2 = (f32[2,128,384]{2,1,0:T(8,128)S(1)}, f32[2,128,384]{2,1,0:T(8,128)S(1)}, u32[]{:S(2)}, u32[]{:S(2)}) collective-permute-start(f32[2,128,384]{2,1,0:T(8,128)S(1)} %get-tuple-element.46), channel_id=1, source_target_pairs={{0,1},{1,2},{2,3},{3,4},{4,5},{5,6},{6,7},{7,0},{32,39},{33,32},{3... | collective-permute-start | bytes 1179656 | tf_op jit(solution)/shard_map/ppermute | solution.py:180
  29.4 5.3 %collective-permute-done.4.half_ref = f32[2,64,384]{2,1,0:T(8,128)S(1)} collective-permute-done((f32[2,64,384]{2,1,0:T(8,128)S(1)}, f32[2,64,384]{2,1,0:T(8,128)S(1)}, u32[]{:S(2)}, u32[]{:S(2)}) %collective-permute-start.4) | collective-permute-done | bytes 196640 | tf_op jit(solution)/shard_map/ppermute | solution.py:180
  34.7 0.0 collective-permute-done.3.third_ref
  34.7 0.1 shard_map.53
  34.7 3.0 %collective-permute-start.5 = (f32[2,128,384]{2,1,0:T(8,128)S(1)}, f32[2,128,384]{2,1,0:T(8,128)S(1)}, u32[]{:S(2)}, u32[]{:S(2)}) collective-permute-start(f32[2,128,384]{2,1,0:T(8,128)S(1)} %shard_map.53), channel_id=1, source_target_pairs={{0,2},{1,3},{2,4},{3,5},{4,6},{5,7},{6,0},{7,1},{32,38},{33,39},{3... | collective-permute-start | bytes 1179656 | tf_op jit(solution)/shard_map/ppermute | solution.py:180
  37.7 2.5 %collective-permute-done.2.a_ref = f32[2,128,384]{2,1,0:T(8,128)S(1)} collective-permute-done((f32[2,128,384]{2,1,0:T(8,128)S(1)}, f32[2,128,384]{2,1,0:T(8,128)S(1)}, u32[]{:S(2)}, u32[]{:S(2)}) %collective-permute-start.2) | collective-permute-done | bytes 393248 | tf_op jit(solution)/shard_map/ppermute | solution.py:180
  40.2 8.5 %collective-permute-done.5.b_ref = f32[2,128,384]{2,1,0:T(8,128)S(1)} collective-permute-done((f32[2,128,384]{2,1,0:T(8,128)S(1)}, f32[2,128,384]{2,1,0:T(8,128)S(1)}, u32[]{:S(2)}, u32[]{:S(2)}) %collective-permute-start.5) | collective-permute-done | bytes 393248 | tf_op jit(solution)/shard_map/ppermute | solution.py:180
  48.8 6.0 %collective-permute-start.6 = (f32[2,128,384]{2,1,0:T(8,128)S(1)}, f32[2,128,384]{2,1,0:T(8,128)S(1)}, u32[]{:S(2)}, u32[]{:S(2)}) collective-permute-start(f32[2,128,384]{2,1,0:T(8,128)S(1)} %shard_map.54.mine_ref), channel_id=1, source_target_pairs={{0,32},{32,0},{1,33},{33,1},{2,34},{34,2},{3,35},{35,3},{4,36},{36... | collective-permute-start | bytes 1179656 | tf_op jit(solution)/shard_map/ppermute | solution.py:188
  54.8 1.3 collective-permute-done.6.received_ref
  56.1 0.1 shard_map.55
  56.2 67.8 %conditional.1 = ((f32[512,384]{1,0:T(8,128)S(1)}, f32[512,384]{1,0:T(8,128)S(1)})) conditional(s32[]{:T(128)} %convert_element_type.3, (bf16[128,384]{1,0:T(8,128)(2,1)S(1)}, bf16[128,384]{1,0:T(8,128)(2,1)S(1)}, bf16[1024,512]{1,0:T(8,128)(2,1)S(1)}, bf16[1024,512]{1,0:T(8,128)(2,1)S(1)}) %tuple.37, (bf16[128,384]{1,0:T(8,128)(2,1)S(1)}, ...), branch_computations={%region_0.0_spmd, %region_1.0_spmd} | conditional | flops 16020000768 | bytes 14680072 | solution.py:339
  56.2 11.2 %all_to_all.28.after_ref.few_ref = bf16[8,32,384]{2,1,0:T(8,128)(2,1)S(1)} all-to-all(bf16[8,32,384]{2,1,0:T(8,128)(2,1)S(1)} %branch_0_fun.5), channel_id=1, replica_groups=mesh['z'=16,'core'=2,'row'=4,'col'=8] {'col'}, dimensions={0} | all-to-all | bytes 393216 | tf_op jit(solution)/shard_map/cond/branch_0_fun/all_to_all | solution.py:174
  67.5 0.1 branch_0_fun.6
  67.6 24.4 %all_to_all.29.many_ref = bf16[8,224,384]{2,1,0:T(8,128)(2,1)S(1)} all-to-all(bf16[8,224,384]{2,1,0:T(8,128)(2,1)S(1)} %branch_0_fun.6), channel_id=1, replica_groups=mesh['z'=16,'core'=2,'row'=4,'col'=8] {'col'}, dimensions={0} | all-to-all | bytes 2752512 | tf_op jit(solution)/shard_map/cond/branch_0_fun/all_to_all | solution.py:174
  91.9 1.3 %branch_0_fun.7 = f32[4,256,384]{2,1,0:T(8,128)S(1)} custom-call(bf16[1024,512]{1,0:T(8,128)(2,1)S(1)} %get-tuple-element.24.mine_ref, bf16[1024,512]{1,0:T(8,128)(2,1)S(1)} %get-tuple-element.25.other_ref, bf16[8,32,384]{2,1,0:T(8,128)(2,1)S(1)} %all_to_all.28.after_ref.few_ref, bf16[8,224,384]{2,1,0:T(8,128)(2,1)S(1)} %all_to_all.29.many_ref), custom_call_target="tpu_custom_call" | custom-call | flops 2000000000 | bytes 1048576 | tf_op jit(solution)/shard_map/cond/branch_0_fun/pallas_call | solution.py:324
  93.3 15.0 %all_to_all.30.parts_ref = f32[4,256,384]{2,1,0:T(8,128)S(1)} all-to-all(f32[4,256,384]{2,1,0:T(8,128)S(1)} %branch_0_fun.7), channel_id=1, replica_groups=mesh['z'=16,'core'=2,'row'=4,'col'=8] {'row'}, dimensions={0} | all-to-all | bytes 3145728 | tf_op jit(solution)/shard_map/cond/branch_0_fun/all_to_all | solution.py:174
  108.3 0.1 branch_0_fun.8
  108.4 15.2 %all_to_all.31.both_ref = f32[4,256,384]{2,1,0:T(8,128)S(1)} all-to-all(f32[4,256,384]{2,1,0:T(8,128)S(1)} %branch_0_fun.8), channel_id=1, replica_groups=mesh['z'=16,'core'=2,'row'=4,'col'=8] {'row'}, dimensions={0} | all-to-all | bytes 3145728 | tf_op jit(solution)/shard_map/cond/branch_0_fun/all_to_all | solution.py:174
  123.7 0.1 branch_0_fun.9
  124.0 6.5 %collective-permute-start.7 = (f32[512,384]{1,0:T(8,128)S(1)}, f32[512,384]{1,0:T(8,128)S(1)}, u32[]{:S(2)}, u32[]{:S(2)}) collective-permute-start(f32[512,384]{1,0:T(8,128)S(1)} %get-tuple-element.59), channel_id=1, source_target_pairs={{0,32},{32,0},{1,33},{33,1},{2,34},{34,2},{3,35},{35,3},{4,36},{36... | collective-permute-start | bytes 2359304 | tf_op jit(solution)/shard_map/ppermute | solution.py:188
  130.5 1.9 %collective-permute-done.7 = f32[512,384]{1,0:T(8,128)S(1)} collective-permute-done((f32[512,384]{1,0:T(8,128)S(1)}, f32[512,384]{1,0:T(8,128)S(1)}, u32[]{:S(2)}, u32[]{:S(2)}) %collective-permute-start.7) | collective-permute-done | bytes 786464 | tf_op jit(solution)/shard_map/ppermute | solution.py:188
  132.4 0.9 slice_select_fusion
  133.3 1.0 broadcast_select_fusion
  (2 shorter events, 0.1 us)
Async XLA Ops:
  0.6 19.9 %collective-permute-start = (bf16[1024,512]{1,0:T(8,128)(2,1)}, bf16[1024,512]{1,0:T(8,128)(2,1)S(1)}, u32[]{:S(2)}, u32[]{:S(2)}) collective-permute-start(bf16[1024,512]{1,0:T(8,128)(2,1)} %refs_0_.3), channel_id=1, source_target_pairs={{0,32},{32,0},{1,33},{33,1},{2,34},{34,2},{3,35},{35,3},{4,36},{36... | collective-permute-start | bytes 3145736 | tf_op jit(solution)/shard_map/ppermute | solution.py:188
  16.7 3.8 %collective-permute-start.1 = (bf16[512,384]{1,0:T(8,128)(2,1)}, bf16[512,384]{1,0:T(8,128)(2,1)S(1)}, u32[]{:S(2)}, u32[]{:S(2)}) collective-permute-start(bf16[512,384]{1,0:T(8,128)(2,1)} %refs_2_.3), channel_id=1, source_target_pairs={{0,32},{32,0},{1,33},{33,1},{2,34},{34,2},{3,35},{35,3},{4,36},{36... | collective-permute-start | bytes 1179656 | tf_op jit(solution)/shard_map/ppermute | solution.py:188
  20.5 1.0 copy-start
  21.5 5.3 %copy-start.1 = (bf16[1024,512]{1,0:T(8,128)(2,1)S(1)}, bf16[1024,512]{1,0:T(8,128)(2,1)}, u32[]{:S(2)}) copy-start(bf16[1024,512]{1,0:T(8,128)(2,1)} %refs_0_.3) | copy-start | bytes 3145732
  23.0 11.7 %collective-permute-start.3 = (f32[2,128,384]{2,1,0:T(8,128)S(1)}, f32[2,128,384]{2,1,0:T(8,128)S(1)}, u32[]{:S(2)}, u32[]{:S(2)}) collective-permute-start(f32[2,128,384]{2,1,0:T(8,128)S(1)} %get-tuple-element.48), channel_id=1, source_target_pairs={{0,1},{1,2},{2,3},{3,4},{4,5},{5,6},{6,7},{7,0},{32,39},{33,32},{3... | collective-permute-start | bytes 1179656 | tf_op jit(solution)/shard_map/ppermute | solution.py:180
  24.9 9.8 %collective-permute-start.4 = (f32[2,64,384]{2,1,0:T(8,128)S(1)}, f32[2,64,384]{2,1,0:T(8,128)S(1)}, u32[]{:S(2)}, u32[]{:S(2)}) collective-permute-start(f32[2,64,384]{2,1,0:T(8,128)S(1)} %get-tuple-element.44.refs_4_), channel_id=1, source_target_pairs={{0,2},{1,3},{2,4},{3,5},{4,6},{5,7},{6,0},{7,1},{32,38},{33,39},{3... | collective-permute-start | bytes 589832 | tf_op jit(solution)/shard_map/ppermute | solution.py:180
  27.4 12.8 %collective-permute-start.2 = (f32[2,128,384]{2,1,0:T(8,128)S(1)}, f32[2,128,384]{2,1,0:T(8,128)S(1)}, u32[]{:S(2)}, u32[]{:S(2)}) collective-permute-start(f32[2,128,384]{2,1,0:T(8,128)S(1)} %get-tuple-element.46), channel_id=1, source_target_pairs={{0,1},{1,2},{2,3},{3,4},{4,5},{5,6},{6,7},{7,0},{32,39},{33,32},{3... | collective-permute-start | bytes 1179656 | tf_op jit(solution)/shard_map/ppermute | solution.py:180
  34.7 14.0 %collective-permute-start.5 = (f32[2,128,384]{2,1,0:T(8,128)S(1)}, f32[2,128,384]{2,1,0:T(8,128)S(1)}, u32[]{:S(2)}, u32[]{:S(2)}) collective-permute-start(f32[2,128,384]{2,1,0:T(8,128)S(1)} %shard_map.53), channel_id=1, source_target_pairs={{0,2},{1,3},{2,4},{3,5},{4,6},{5,7},{6,0},{7,1},{32,38},{33,39},{3... | collective-permute-start | bytes 1179656 | tf_op jit(solution)/shard_map/ppermute | solution.py:180
  48.8 7.4 %collective-permute-start.6 = (f32[2,128,384]{2,1,0:T(8,128)S(1)}, f32[2,128,384]{2,1,0:T(8,128)S(1)}, u32[]{:S(2)}, u32[]{:S(2)}) collective-permute-start(f32[2,128,384]{2,1,0:T(8,128)S(1)} %shard_map.54.mine_ref), channel_id=1, source_target_pairs={{0,32},{32,0},{1,33},{33,1},{2,34},{34,2},{3,35},{35,3},{4,36},{36... | collective-permute-start | bytes 1179656 | tf_op jit(solution)/shard_map/ppermute | solution.py:188
  124.0 8.4 %collective-permute-start.7 = (f32[512,384]{1,0:T(8,128)S(1)}, f32[512,384]{1,0:T(8,128)S(1)}, u32[]{:S(2)}, u32[]{:S(2)}) collective-permute-start(f32[512,384]{1,0:T(8,128)S(1)} %get-tuple-element.59), channel_id=1, source_target_pairs={{0,32},{32,0},{1,33},{33,1},{2,34},{34,2},{3,35},{35,3},{4,36},{36... | collective-permute-start | bytes 2359304 | tf_op jit(solution)/shard_map/ppermute | solution.py:188
